TPU v7x, 32 devices: a whole 2x2x4 slice. The times are simulated.
32 devices in a mesh: stn: 8 (over z, y), grid: 4 (over x, core).
Axes of the slice: x: 2, y: 2, z: 4, core: 2. Of those that a mesh axis runs over, the one named last changes fastest.
Arguments:
- voltages: bfloat16 [512, 2, 12288], P('stn', None, 'grid'), may hold values from -6 to 6
- pfb_coeffs: float32 [16, 48], replicated, may hold values from -1.5 to 1.5
- station_offsets: int32 [2, 512], replicated, may hold values from 0 to 4
- tile_cells: int32 [24, 2, 136], P('stn'), may hold values from 0 to 127, as said below
- kernel_table: float32 [8, 7], replicated, may hold values from 0.2 to 1
Outputs:
- uv_grid: float32 [128, 24, 256], P('grid', 'stn')
Inputs may be any that keep to these rules, and one draw needn't show every extreme that they name: tile_cells[c, 0, k] lies in one of the strips of 32 rows; in every channel at most 68 baseline tiles have their base row in the same strip, and one strip holds exactly 68. A base row in the last strip and every base column are at most 112.
All inputs are finite; a program needn't handle non-finite values.
Results may differ from a plain program's by a relative error of at most 0.0065.
Values may be sent and summed in bfloat16 or wider, within the bound.
A program may use at most 128 MiB of HBM per device.

v0:
```python
import functools
import math

import jax
import jax.numpy as jnp
import numpy as np
from jax import lax
from jax.experimental import pallas as pl
from jax.experimental.pallas import tpu as pltpu
from jax.sharding import PartitionSpec as P

TILE = 32
PATCH = 16
SPREAD = 5
UV = 128


highest = lax.Precision.HIGHEST


def shifted(block, axis, distance):
    devices = range(lax.axis_size(axis))
    route = [(i - distance, i) for i in devices if i - distance in devices]
    return lax.ppermute(block, axis, route)


def dft_table(frame_len):
    chan_count = frame_len // 2
    sample_line = jnp.arange(frame_len, dtype=jnp.int32)[:, None]
    chan_line = jnp.arange(chan_count, dtype=jnp.int32)[None, :]
    angles = (sample_line * chan_line % frame_len).astype(jnp.float32) * (2.0 * math.pi / frame_len)
    norm_factor = 1.0 / math.sqrt(frame_len)
    twiddle = jnp.stack([jnp.cos(angles) * norm_factor, -jnp.sin(angles) * norm_factor], axis=2)
    return twiddle.reshape(frame_len, 2 * chan_count).astype(jnp.bfloat16)


CLASSES = SPREAD * SPREAD
high = lax.Precision.HIGH


def fused_filter(coeffs, twiddle, step):
    taps, frame_len = coeffs.shape
    flat = coeffs.reshape(-1)
    columns = [
        jnp.pad(flat, (frame_len * (f + 1), frame_len * (step - 1 - f))) for f in range(step)
    ]
    shifted_coeffs = jnp.stack(columns, axis=0)
    spread = np.kron(np.ones((1, frame_len), np.float32), np.eye(step, dtype=np.float32))
    wide = jnp.einsum("fm,fn->mn", shifted_coeffs, jnp.asarray(spread), precision=highest)
    tiled = jnp.tile(jnp.repeat(twiddle.astype(jnp.float32), step, axis=1), (step + taps, 1))
    return (wide * tiled).astype(jnp.bfloat16)

def separation_table(frequency, divisor, kernel_table):
    over_count = kernel_table.shape[0]
    separation = jnp.arange(2 * SPREAD - 1, dtype=jnp.int32)
    scaled = separation * frequency
    cell_index = scaled // divisor
    fine_index = scaled % divisor * over_count // divisor
    choose = (fine_index[:, None] == jnp.arange(over_count, dtype=jnp.int32)[None, :]).astype(
        jnp.float32
    )
    tap_values = jnp.dot(choose, kernel_table, precision=highest)
    place_rel = jnp.arange(PATCH, dtype=jnp.int32)[None, :] - cell_index[:, None]
    weights = jnp.zeros(place_rel.shape, jnp.float32)
    for tap_index in range(kernel_table.shape[1]):
        weights = weights + tap_values[:, tap_index : tap_index + 1] * (
            place_rel == tap_index
        ).astype(jnp.float32)
    return weights


def shifted_weights(weights, bases):
    place = jnp.arange(UV, dtype=jnp.int32)[None, :, None] - bases[:, None, :]
    taps = jnp.arange(PATCH, dtype=jnp.int32)[None, :, None, None]
    spots = place[:, None] == taps
    if weights.dtype == jnp.float32:
        return jnp.einsum("cdt,ctwp->cdwp", weights, spots.astype(jnp.float32), precision=highest)
    return jnp.einsum(
        "cdt,ctwp->cdwp", weights, spots.astype(jnp.bfloat16), preferred_element_type=jnp.float32
    ).astype(jnp.bfloat16)


def body(voltages, pfb_coeffs, station_offsets, tile_cells, kernel_table):
    stn_local, pol_count, samples = voltages.shape
    tap_count, frame_len = pfb_coeffs.shape
    spec_count = samples // frame_len
    step = 128 // math.gcd(128, frame_len)
    chunks = spec_count // step
    flat = jnp.transpose(voltages, (1, 0, 2))
    earlier = shifted(flat[:, :, samples - tap_count * frame_len :], "grid", 1)
    extended = jnp.concatenate([earlier, flat], axis=2)
    width = step * frame_len
    reach = (step + tap_count) * frame_len
    blocks = jnp.stack(
        [extended[:, :, c * width : c * width + reach] for c in range(chunks)], axis=1
    )
    matrix = fused_filter(pfb_coeffs, dft_table(frame_len), step)
    spectra = jnp.einsum(
        "pcsm,mn->npcs", blocks, matrix, preferred_element_type=jnp.float32
    ).astype(jnp.bfloat16)
    spectra = spectra.reshape(frame_len // 2, 2, step * pol_count * chunks, stn_local)
    spectra, tile_cells = lax.optimization_barrier((spectra, tile_cells))
    turned = lax.all_to_all(spectra, "stn", split_axis=0, concat_axis=3, tiled=True)
    turned = jnp.transpose(turned, (0, 1, 3, 2))
    ch_dev, _, stations, depth = turned.shape
    tiles = stations // TILE
    divisor = frame_len - 1
    first_chan = lax.axis_index("stn") * ch_dev + frame_len // 2
    norm_factor = 1.0 / (pol_count * spec_count * lax.axis_size("grid"))

    classes = (station_offsets[0] * SPREAD + station_offsets[1]).reshape(tiles, TILE)
    hot = classes[:, :, None] == jnp.arange(CLASSES, dtype=jnp.int32)
    hot_low = hot.astype(jnp.bfloat16)
    hot_full = hot.astype(jnp.float32)
    tiled = turned.reshape(ch_dev, 2, tiles, TILE, depth)
    summed = jnp.einsum(
        "aiq,ceaik->ceaqk", hot_low, tiled, preferred_element_type=jnp.float32
    ).astype(jnp.bfloat16)

    def stacked(z):
        real_part, imag_part = z[:, 0], z[:, 1]
        partner = jnp.concatenate([real_part, imag_part], axis=-1)
        turned_partner = jnp.concatenate([imag_part, -real_part], axis=-1)
        return jnp.stack([partner, turned_partner], axis=1), partner

    left, right = stacked(summed)
    shape = (SPREAD, SPREAD, 2 * depth)
    terms = []
    for i in range(ch_dev):
        taps = jnp.transpose(left[i].reshape((2 * tiles,) + shape), (1, 2, 3, 0))
        terms.append(
            lax.conv_general_dilated(
                right[i].reshape((tiles,) + shape),
                taps,
                (1, 1),
                [(SPREAD - 1, SPREAD - 1)] * 2,
                dimension_numbers=("NHWC", "HWIO", "HWNC"),
                preferred_element_type=jnp.float32,
            )
        )
    seps = 2 * SPREAD - 1
    cross = jnp.stack(terms).reshape(ch_dev, seps, seps, tiles, 2, tiles)
    cross = jnp.transpose(cross, (0, 4, 1, 2, 3, 5)).reshape(ch_dev, 2, seps, seps, tiles * tiles)
    own_left, own_right = stacked(tiled)
    own = jnp.einsum("ceaik,cajk->ceaij", own_left, own_right, preferred_element_type=jnp.float32)
    line = np.arange(TILE)
    own = jnp.where(jnp.asarray(line[:, None] < line[None, :]), own, 0.0)
    own = jnp.einsum("aiq,ceaij->ceaqj", hot_full, own, precision=high)
    own = jnp.einsum("ceaqj,ajs->ceasq", own, hot_full, precision=high)
    class_line = np.arange(CLASSES)
    back_u = class_line[:, None] // SPREAD - class_line[None, :] // SPREAD + SPREAD - 1
    back_v = class_line[:, None] % SPREAD - class_line[None, :] % SPREAD + SPREAD - 1
    pick = np.arange(seps * seps) == (back_u * seps + back_v).reshape(-1, 1)
    own = jnp.einsum(
        "ceam,mz->ceza",
        own.reshape(ch_dev, 2, tiles, CLASSES * CLASSES),
        jnp.asarray(pick.astype(np.float32)),
        precision=high,
    )
    diagonal = np.zeros((tiles, tiles * tiles), np.float32)
    diagonal[np.arange(tiles), np.arange(tiles) * (tiles + 1)] = 1.0
    own = jnp.einsum("ceza,ap->cezp", own, jnp.asarray(diagonal), precision=high)
    own = own.reshape(ch_dev, 2, seps, seps, tiles * tiles)
    same = jnp.asarray(diagonal.sum(axis=0) > 0)
    cross = jnp.where(same, own, cross)

    pair_first, pair_second = np.triu_indices(tiles)
    select = np.zeros((pair_first.size, tiles * tiles), np.float32)
    select[np.arange(pair_first.size), pair_second * tiles + pair_first] = 1.0
    missing = (1.0 - select.sum(axis=0)).astype(np.int32) * 4096
    cells = jnp.einsum(
        "cxk,kp->cxp", tile_cells.astype(jnp.float32), jnp.asarray(select), precision=highest
    )
    cells = jnp.round(cells).astype(jnp.int32) + jnp.asarray(missing)
    weights = jnp.stack(
        [separation_table(first_chan + i, divisor, kernel_table)[::-1] for i in range(ch_dev)]
    )
    scaled = weights * norm_factor
    coarse = lax.reduce_precision(scaled, 8, 7)
    rest = (scaled - coarse).astype(jnp.bfloat16)
    rows = [shifted_weights(part, cells[:, 0]) for part in (coarse.astype(jnp.bfloat16), rest)]
    place = jnp.arange(UV, dtype=jnp.int32)[None, :, None] - cells[:, 1][:, None, :]
    cols = []
    for v in range(seps):
        placed = jnp.zeros(place.shape, jnp.float32)
        for t in range(PATCH):
            placed = jnp.where(place == t, weights[:, v, t][:, None, None], placed)
        cols.append(placed)
    cols = lax.optimization_barrier(tuple(cols))
    spread_cols = sum(
        cross[:, :, :, v, None, :] * cols[v][:, None, None] for v in range(seps)
    )
    spread_cols = spread_cols.astype(jnp.bfloat16)
    planes = sum(
        jnp.einsum(
            "cdup,cedwp->ucew", part, spread_cols, preferred_element_type=jnp.float32
        )
        for part in rows
    )
    grid_count = lax.axis_size("grid")
    planes = planes.reshape(grid_count, UV // grid_count, ch_dev, 2 * UV).astype(jnp.bfloat16)
    parts = lax.all_to_all(planes, "grid", split_axis=0, concat_axis=0, tiled=True)
    return parts.astype(jnp.float32).sum(axis=0)


f32, bf16, i32 = jnp.float32, jnp.bfloat16, jnp.int32
MESH = pl.DeviceIdType.MESH
SEPS = 2 * SPREAD - 1
STEP = 16
ROWS = 112
LANES = 128
PAIR_ROWS = 256


def iota(shape, axis):
    return lax.broadcasted_iota(i32, shape, axis)


def ones_where(mask, kind=bf16):
    return jnp.where(mask, 1.0, 0.0).astype(kind)


def dot(a, b):
    return lax.dot_general(a, b, (((1,), (0,)), ((), ())), preferred_element_type=f32)


def dot_nt(a, b):
    return lax.dot_general(a, b, (((1,), (1,)), ((), ())), preferred_element_type=f32)


def split(x):
    top = x.astype(bf16)
    return top, (x - top.astype(f32)).astype(bf16)


def send_order(n):
    return sorted(range(1, n), key=lambda k: abs(2 * k - n))


def front_kernel(
    dims, v_ref, coef_ref, tw_ref, off_ref, off_smem, recv_ref, drecv_ref,
    vext, wide, spec, send, own, vis, left, picks, dsend,
    in_sem, halo_send, halo_recv, send_sem, recv_sem, dsend_sem, drecv_sem,
):
    n_stn, n_grid, chans, taps, frame_len, st = dims
    me, here = lax.axis_index("stn"), lax.axis_index("grid")
    reach = (STEP + taps) * frame_len
    halo = taps * frame_len
    samples = v_ref.shape[1]
    blocks = samples // (STEP * frame_len)
    order = send_order(n_stn)

    barrier = pltpu.get_barrier_semaphore()
    for k in range(1, n_stn):
        pl.semaphore_signal(
            barrier, inc=1, device_id=(lax.rem(me + k, n_stn), here), device_id_type=MESH
        )
    for k in range(1, n_grid):
        pl.semaphore_signal(
            barrier, inc=1, device_id=(me, lax.rem(here + k, n_grid)), device_id_type=MESH
        )
    load = pltpu.make_async_copy(v_ref, vext.at[:, pl.ds(halo, samples)], in_sem)
    load.start()

    coef = coef_ref[...]
    line = jnp.concatenate(
        [jnp.zeros((1, frame_len), f32)]
        + [coef[k : k + 1, :] for k in range(taps)]
        + [jnp.zeros((1, reach - (taps + 1) * frame_len), f32)],
        axis=1,
    )
    shifted_line = jnp.concatenate(
        [line if f == 0 else pltpu.roll(line, f * frame_len, 1) for f in range(STEP)], axis=0
    )
    for r in range(2 * n_stn * chans):
        wide[r * STEP : (r + 1) * STEP, :] = (tw_ref[r : r + 1, :] * shifted_line).astype(bf16)

    offs = off_ref[...].astype(f32)
    stations = offs.shape[1]
    cls = jnp.broadcast_to(SPREAD * offs[0:1] + offs[1:2], (16, stations)).astype(bf16)
    kap = jnp.broadcast_to(SEPS * offs[0:1] + offs[1:2], (LANES, stations)).astype(bf16)
    row_of = (stations, LANES)
    mine = ones_where(iota(row_of, 0) == me * st + iota(row_of, 1) // 2)
    cls_line = dot(cls, mine)[0:1]
    lane = iota((1, LANES), 1)
    code = ((lane % 2) * 2 + lane // 2 // TILE).astype(f32) * CLASSES + cls_line
    line_a = iota((ROWS, LANES), 0).astype(f32)
    sum_rows = ones_where(line_a == code)
    line_b = iota((LANES, LANES), 0)
    lane_b = iota((LANES, LANES), 1)
    own_rows = ones_where(line_b == (lane_b % 2) * st + lane_b // 2)
    gather_rows = jnp.concatenate([sum_rows, own_rows], axis=0)

    pl.semaphore_wait(barrier, n_stn + n_grid - 2)

    @pl.when(here < n_grid - 1)
    def _():
        pltpu.make_async_remote_copy(
            src_ref=v_ref.at[:, pl.ds(samples - halo, halo)],
            dst_ref=vext.at[:, pl.ds(0, halo)],
            send_sem=halo_send,
            recv_sem=halo_recv,
            device_id=(me, here + 1),
            device_id_type=MESH,
        ).start()

    load.wait()

    def filtered(c, t):
        rows = wide[c * 2 * n_stn * STEP : (c + 1) * 2 * n_stn * STEP, :]
        window = vext[:, t * STEP * frame_len : t * STEP * frame_len + reach]
        got = dot_nt(rows, window).astype(bf16)
        spec[c, :, :, t] = got.reshape(n_stn, 2, STEP, LANES)

    for t in range(1, blocks):
        filtered(0, t)

    halo_copy = pltpu.make_async_remote_copy(
        src_ref=v_ref.at[:, pl.ds(samples - halo, halo)],
        dst_ref=vext.at[:, pl.ds(0, halo)],
        send_sem=halo_send,
        recv_sem=halo_recv,
        device_id=(me, lax.rem(here + 1, n_grid)),
        device_id_type=MESH,
    )

    @pl.when(here > 0)
    def _():
        halo_copy.wait_recv()

    @pl.when(here == 0)
    def _():
        vext[:, 0:halo] = jnp.zeros((LANES, halo), bf16)

    copies = []
    for c in range(chans):
        for t in range(blocks) if c else (0,):
            filtered(c, t)
        for k in order + [0]:
            to = lax.rem(me + k, n_stn)
            got = dot_nt(gather_rows, spec[c, to].reshape(LANES, LANES))
            send[c, to] = got[:ROWS].astype(bf16)
            alone = got[ROWS:].astype(bf16)
            own[c, to] = jnp.concatenate([alone[:st], alone[st:]], axis=1)
            if k:
                copy = pltpu.make_async_remote_copy(
                    src_ref=send.at[c, to],
                    dst_ref=recv_ref.at[c, me],
                    send_sem=send_sem.at[c, k],
                    recv_sem=recv_sem.at[c, k],
                    device_id=(to, here),
                    device_id_type=MESH,
                )
                copy.start()
                copies.append(copy)
            else:
                recv_ref[c, me] = send[c, me]

    vis[...] = jnp.zeros(vis.shape, f32)
    lane2 = iota((st, 2 * LANES), 1)
    flip = jnp.where(lane2 % LANES < LANES // 2, 1.0, -1.0)
    for c in range(chans):
        for d in range(n_stn):
            x = own[c, d]
            xf = x.astype(f32)
            turned = jnp.concatenate(
                [
                    pltpu.roll(xf[:, p * LANES : (p + 1) * LANES], LANES // 2, 1)
                    for p in range(2)
                ],
                axis=1,
            )
            both = jnp.concatenate([x, (turned * flip).astype(bf16)], axis=0)
            got = dot_nt(both, jnp.concatenate([x, x], axis=0))
            for e in range(2):
                vis[d * 8 + c * 2 + e] = got[e * st : (e + 1) * st]

    half = n_stn * 8
    lane3 = iota((half, LANES), 1)
    for k in range(TILE // 2):
        even = jnp.where(lane3 % st < TILE, vis[:, 2 * k, :], vis[:, 2 * k + TILE, :])
        odd = jnp.where(lane3 % st < TILE, vis[:, 2 * k + 1, :], vis[:, 2 * k + 1 + TILE, :])
        top, low = split(jnp.where(lane3 < st, even, odd))
        left[0:half, k * LANES : (k + 1) * LANES] = top
        left[half:, k * LANES : (k + 1) * LANES] = low
    which = (st, stations)
    kap_col = dot_nt(ones_where(iota(which, 1) == me * st + iota(which, 0)), kap)
    base = kap_col.astype(i32) + iota((st, LANES), 1) - (SEPS * (SPREAD - 1) + SPREAD - 1)
    blank = jnp.zeros((TILE, LANES), bf16)
    row_t = iota((TILE, LANES), 0)
    for i in range(TILE):
        for a in range(2):
            at = me * st + a * TILE + i
            value = off_smem[0, at] * SEPS + off_smem[1, at]
            hit = ones_where((base[a * TILE : (a + 1) * TILE] == value) & (row_t > i))
            first = i * st + a * TILE
            picks[first : first + TILE, a * LANES : (a + 1) * LANES] = hit
            picks[first : first + TILE, (1 - a) * LANES : (2 - a) * LANES] = blank
    binned = dot(left[...], picks[...])
    binned = (binned[:half] + binned[half:]).reshape(n_stn, 8, 2 * LANES)
    dsend[...] = binned
    for k in order:
        to = lax.rem(me + k, n_stn)
        copy = pltpu.make_async_remote_copy(
            src_ref=dsend.at[to],
            dst_ref=drecv_ref.at[me],
            send_sem=dsend_sem.at[k],
            recv_sem=drecv_sem.at[k],
            device_id=(to, here),
            device_id_type=MESH,
        )
        copy.start()
        copies.append(copy)
    drecv_ref[me] = dsend[me]

    for copy in copies:
        copy.wait()

    @pl.when(here < n_grid - 1)
    def _():
        halo_copy.wait_send()


def back_kernel(
    dims, recv_ref, drecv_ref, cells_ref, table_ref, out_ref,
    perm, bands, vweights, xs, sums, placed,
):
    n_stn, n_grid, chans, taps, frame_len, st = dims
    me = lax.axis_index("stn")
    tiles = 2 * n_stn
    over, kern = table_ref.shape
    divisor = frame_len - 1
    side = SPREAD * tiles
    full = SPREAD * side
    depth = 2 * LANES
    wide = tiles * PATCH

    shape = (perm.shape[1], perm.shape[2])
    r, col = iota(shape, 0), iota(shape, 1)
    b, q = r % tiles, r // tiles
    for p in range(2):
        want = (b // 2) * ROWS + (p * 2 + b % 2) * CLASSES + q
        perm[p] = ones_where((col == want) & (r < full))

    npair = cells_ref.shape[2]

    def pair_number(a, b):
        return jnp.where(a <= b, a * tiles - a * (a - 1) // 2 + b - a, -1)

    kl = (npair, PAIR_ROWS)
    choose = ones_where(iota(kl, 0) == pair_number(iota(kl, 1) // tiles, iota(kl, 1) % tiles))
    kr = (PAIR_ROWS, npair)
    choose_t = ones_where(iota(kr, 1) == pair_number(iota(kr, 0) // tiles, iota(kr, 0) % tiles))
    lane_pair = iota((1, PAIR_ROWS), 1)
    absent = jnp.where(lane_pair // tiles <= lane_pair % tiles, 0.0, -1000.0)

    def weight_rows(c, d, r):
        scaled = (d * (me * chans + c + frame_len // 2)).astype(f32)
        cell = jnp.floor((scaled + 0.5) / divisor)
        rest = scaled - cell * divisor
        fine = jnp.floor((rest * over + 0.5) / divisor)
        tap = r - cell.astype(i32)
        code = jnp.where((tap >= 0) & (tap < kern), fine.astype(i32) * kern + tap, -1)
        got = jnp.zeros(code.shape, f32)
        for o in range(over):
            for t in range(kern):
                got = jnp.where(code == o * kern + t, table_ref[o, t], got)
        return got

    placed[...] = jnp.zeros(placed.shape, bf16)
    norm = 1.0 / (n_grid * depth // 2)
    rows_t = (16, UV)
    rows_w = (16, wide)
    same_tile = iota((tiles, wide), 0) == iota((tiles, wide), 1) // PATCH
    own_lane = iota((32, LANES), 1) // SEPS
    lane_p = (2 * tiles, LANES)
    for c in range(chans):
        cells = cells_ref[c].astype(f32)
        row_line = dot(jnp.broadcast_to(cells[0:1], (16, npair)).astype(bf16), choose)[0:1] + absent
        col_rows = dot_nt(choose_t, jnp.broadcast_to(cells[1:2], (LANES, npair)).astype(bf16))
        spot = iota((UV, PAIR_ROWS), 0).astype(f32) == row_line
        spots = ones_where(spot)
        lines = weight_rows(c, iota(rows_t, 0), (UV - iota(rows_t, 1)) % UV)
        for du in range(SEPS):
            band = pltpu.roll(
                jnp.broadcast_to(lines[du : du + 1], (UV, UV)), 0, 1, stride=1, stride_axis=0
            )
            top, low = split(band)
            bands[c, du] = dot(jnp.concatenate([top, low], axis=0), spots).astype(bf16)
        across = weight_rows(c, iota(rows_w, 0), iota(rows_w, 1) % PATCH)
        for s in range(SPREAD):
            for q in range(SPREAD):
                at = q - s + SPREAD - 1
                part = jnp.where(same_tile, across[at : at + 1], 0.0)
                top, low = split(part)
                vweights[0, s, q * tiles : (q + 1) * tiles, :] = top
                vweights[1, s, q * tiles : (q + 1) * tiles, :] = low
            vweights[0, s, side:, :] = jnp.zeros((LANES - side, wide), bf16)
            vweights[1, s, side:, :] = jnp.zeros((LANES - side, wide), bf16)
        onto = ones_where(iota((LANES, 16), 0) % SEPS == iota((LANES, 16), 1))
        a_top, a_low = split(across)
        own_top, own_low = dot(onto, a_top).astype(bf16), dot(onto, a_low).astype(bf16)

        got = recv_ref[c].reshape(n_stn * ROWS, LANES)
        lane_h = iota((full, LANES), 1) < LANES // 2
        turned = []
        for p in range(2):
            x = dot(perm[p], got)
            xs[:, p * LANES : (p + 1) * LANES] = x.astype(bf16)
            y = pltpu.roll(x[:full], LANES // 2, 1)
            turned.append(jnp.where(lane_h, -y, y).astype(bf16))
        lefts = [xs[:full], jnp.concatenate(turned, axis=1)]
        for e in range(2):
            blocks = [dot_nt(lefts[e], xs[q * side : q * side + LANES]) for q in range(SPREAD)]
            for du in range(SEPS):
                d = du - (SPREAD - 1)
                total = sum(
                    blocks[s + d][s * side : (s + 1) * side]
                    for s in range(SPREAD)
                    if 0 <= s + d < SPREAD
                )
                top, low = split(total)
                at = (e * SEPS + du) * tiles
                for s in range(SPREAD):
                    sums[0, s, at : at + tiles, :] = top[s * tiles : (s + 1) * tiles]
                    sums[1, s, at : at + tiles, :] = low[s * tiles : (s + 1) * tiles]
        patches = jnp.zeros((2 * SEPS * tiles, wide), f32)
        for s in range(SPREAD):
            for i, j in ((0, 0), (1, 0), (0, 1)):
                patches = patches + dot(sums[i, s], vweights[j, s])

        rr, cc = iota((32, n_stn * 8), 0), iota((32, n_stn * 8), 1)
        take = ones_where(cc == (rr % tiles // 2) * 8 + c * 2 + rr // tiles)
        d_top, d_low = split(drecv_ref[...].reshape(n_stn * 8, 2 * LANES))
        own = dot(take, d_top) + dot(take, d_low)
        odd = iota((32, LANES), 0) % 2 == 1
        own = jnp.where(odd, own[:, LANES:], own[:, :LANES])
        own_parts = []
        for e in range(2):
            for du in range(SEPS):
                own_parts.append(
                    jnp.where(own_lane == du, own, 0.0)[e * tiles : (e + 1) * tiles]
                )
        own_all = jnp.concatenate(own_parts, axis=0)
        o_top, o_low = split(own_all)
        own_patch = dot(o_top, own_top) + dot(o_low, own_top) + dot(o_top, own_low)
        rr, cc = iota(patches.shape, 0), iota(patches.shape, 1)
        patches = jnp.where(rr % tiles == cc // PATCH, own_patch, patches)

        for a in range(tiles):
            low_rows = 8 if a >= 8 else 0
            distance = iota((tiles, LANES), 1) - col_rows[a * tiles : (a + 1) * tiles].astype(i32)
            distance = distance[low_rows:]
            valid = (distance >= 0) & (distance < PATCH)
            index = jnp.where(valid, distance + (a % 8) * PATCH, 0)
            for du in range(SEPS):
                for e in range(2):
                    at = (e * SEPS + du) * tiles
                    source = patches[
                        at + low_rows : at + tiles, a // 8 * LANES : (a // 8 + 1) * LANES
                    ]
                    moved = jnp.where(valid, jnp.take_along_axis(source, index, axis=1), 0.0)
                    if low_rows:
                        moved = jnp.concatenate([jnp.zeros((8, LANES), f32), moved], axis=0)
                    placed[du, a * tiles : (a + 1) * tiles, e * LANES : (e + 1) * LANES] = (
                        moved.astype(bf16)
                    )
        plane = jnp.zeros((2 * UV, 2 * UV), f32)
        for du in range(SEPS):
            plane = plane + dot(bands[c, du], placed[du])
        plane = (plane[:UV] + plane[UV:]) * norm
        out_ref[c] = plane.astype(bf16)


def kernel_body(voltages, pfb_coeffs, station_offsets, tile_cells, kernel_table):
    st, pols, samples = voltages.shape
    taps, frame_len = pfb_coeffs.shape
    n_stn, n_grid = lax.axis_size("stn"), lax.axis_size("grid")
    chans = tile_cells.shape[0]
    dims = (n_stn, n_grid, chans, taps, frame_len, st)
    reach = (STEP + taps) * frame_len
    blocks = samples // (STEP * frame_len)

    table = dft_table(frame_len).astype(f32).T.reshape(n_stn, chans, 2, frame_len)
    table = jnp.transpose(table, (1, 0, 2, 3)).reshape(-1, frame_len)
    table = jnp.tile(table, (1, STEP + taps))
    vmem = pl.BlockSpec(memory_space=pltpu.VMEM)
    smem = pl.BlockSpec(memory_space=pltpu.SMEM)
    anywhere = pl.BlockSpec(memory_space=pl.ANY)
    flat = voltages.reshape(st * pols, samples)
    recv, drecv = pl.pallas_call(
        functools.partial(front_kernel, dims),
        out_shape=[
            jax.ShapeDtypeStruct((chans, n_stn, ROWS, LANES), bf16),
            jax.ShapeDtypeStruct((n_stn, 8, 2 * LANES), f32),
        ],
        in_specs=[anywhere, vmem, vmem, vmem, smem],
        out_specs=[vmem, vmem],
        scratch_shapes=[
            pltpu.VMEM((LANES, taps * frame_len + samples), bf16),
            pltpu.VMEM((2 * n_stn * chans * STEP, reach), bf16),
            pltpu.VMEM((chans, n_stn, 2, blocks, STEP, LANES), bf16),
            pltpu.VMEM((chans, n_stn, ROWS, LANES), bf16),
            pltpu.VMEM((chans, n_stn, st, 2 * LANES), bf16),
            pltpu.VMEM((n_stn * 8, st, LANES), f32),
            pltpu.VMEM((n_stn * 16, TILE * st), bf16),
            pltpu.VMEM((TILE * st, 2 * LANES), bf16),
            pltpu.VMEM((n_stn, 8, 2 * LANES), f32),
            pltpu.SemaphoreType.DMA,
            pltpu.SemaphoreType.DMA,
            pltpu.SemaphoreType.DMA,
            pltpu.SemaphoreType.DMA((chans, n_stn)),
            pltpu.SemaphoreType.DMA((chans, n_stn)),
            pltpu.SemaphoreType.DMA((n_stn,)),
            pltpu.SemaphoreType.DMA((n_stn,)),
        ],
        compiler_params=pltpu.CompilerParams(
            collective_id=0, has_side_effects=True, vmem_limit_bytes=48 << 20
        ),
    )(flat, pfb_coeffs, table, station_offsets, station_offsets)

    tiles = 2 * n_stn
    full = SPREAD * SPREAD * tiles
    planes = pl.pallas_call(
        functools.partial(back_kernel, dims),
        out_shape=jax.ShapeDtypeStruct((chans, UV, 2 * UV), bf16),
        in_specs=[vmem, vmem, vmem, smem],
        out_specs=vmem,
        scratch_shapes=[
            pltpu.VMEM((2, full + 48, n_stn * ROWS), bf16),
            pltpu.VMEM((chans, SEPS, 2 * UV, PAIR_ROWS), bf16),
            pltpu.VMEM((2, SPREAD, LANES, tiles * PATCH), bf16),
            pltpu.VMEM((full + 48, 2 * LANES), bf16),
            pltpu.VMEM((2, SPREAD, 2 * SEPS * tiles, LANES), bf16),
            pltpu.VMEM((SEPS, PAIR_ROWS, 2 * UV), bf16),
        ],
        compiler_params=pltpu.CompilerParams(vmem_limit_bytes=48 << 20),
    )(recv, drecv, tile_cells, kernel_table)
    planes = planes.reshape(chans, n_grid, UV // n_grid, 2 * UV)
    parts = lax.all_to_all(planes, "grid", split_axis=1, concat_axis=1, tiled=True)
    return jnp.transpose(parts.astype(f32).sum(axis=1), (1, 0, 2))


def kernels_fit(mesh, args):
    voltages, pfb_coeffs, offsets, cells, _ = args
    n_stn, n_grid = mesh.shape["stn"], mesh.shape["grid"]
    stations, pols, samples = voltages.shape
    taps, frame_len = pfb_coeffs.shape
    spectra = samples // frame_len // n_grid
    return (
        stations == 2 * TILE * n_stn
        and n_stn == 8
        and pols == 2
        and spectra == 64
        and taps == 16
        and frame_len // 2 == cells.shape[0] == 3 * n_stn
    )


def solution(mesh):
    placed = (P("stn", None, "grid"), P(), P(), P("stn", None, None), P())

    def run(*args):
        inner = kernel_body if kernels_fit(mesh, args) else body
        return jax.shard_map(
            inner, mesh=mesh, in_specs=placed, out_specs=P("grid", "stn", None), check_vma=False
        )(*args)

    return run
```

profile of v0, /device:TPU:0, one launch (start us, length us, event | category | flops | bytes accessed | tf_op | source)
XLA Modules:
  0.0 50.4 jit_solution(6955666657063062675)
XLA Ops:
  0.0 0.1 multiply_convert_fusion
  0.1 0.0 copy-start.4
  0.1 0.1 tile.14
  0.2 0.4 tile.15.tw_ref
  0.7 0.6 %copy-done.4 = bf16[64,2,3072]{2,1,0:T(2,128)(2,1)S(1)} copy-done((bf16[64,2,3072]{2,1,0:T(2,128)(2,1)S(1)}, bf16[64,2,3072]{2,1,0:T(2,128)(2,1)}, u32[]{:S(2)}) %copy-start.4) | copy-done | bytes 786456
  1.3 0.0 copy-start
  1.3 0.0 copy-start.1
  1.3 0.3 reshape.81.v_ref
  1.6 0.4 copy-done
  2.0 0.0 copy-done.1
  2.0 0.0 copy-start.2
  2.0 0.0 copy-start.3
  2.0 26.9 %shard_map.55 = (bf16[3,8,112,128]{3,2,1,0:T(8,128)(2,1)S(1)}, f32[8,8,256]{2,1,0:T(8,128)S(1)}) custom-call(bf16[128,3072]{1,0:T(8,128)(2,1)S(1)} %reshape.81.v_ref, f32[16,48]{1,0:T(8,128)S(1)} %copy-done.1, f32[48,1536]{1,0:T(8,128)S(1)} %tile.15.tw_ref, s32[2,512]{1,0:T(2,128)S(1)} %copy-done, s32[2,512]{1,0:T(2,128)S(1)} %copy-done), custom_call_target="tpu_custom_call" | custom-call | tf_op jit(solution)/shard_map/pallas_call | solution.py:591
  28.9 0.0 copy-done.2
  28.9 0.0 copy-done.3
  28.9 12.9 %shard_map.56 = bf16[3,128,256]{2,1,0:T(8,128)(2,1)S(1)} custom-call(bf16[3,8,112,128]{3,2,1,0:T(8,128)(2,1)S(1)} %get-tuple-element.7.recv_ref, f32[8,8,256]{2,1,0:T(8,128)S(1)} %get-tuple-element.8.drecv_ref, s32[3,2,136]{2,1,0:T(2,128)S(1)} %copy-done.2, f32[8,7]{1,0:T(8,128)S(1)} %copy-done.3), custom_call_target="tpu_custom_call" | custom-call | tf_op jit(solution)/shard_map/pallas_call | solution.py:624
  41.8 8.0 %all_to_all.5 = bf16[3,4,32,256]{3,2,0,1:T(8,128)(2,1)S(1)} all-to-all(bf16[3,4,32,256]{3,2,0,1:T(8,128)(2,1)S(1)} %copy.11), channel_id=1, replica_groups=mesh['stn'=8,'grid'=4] {'grid'}, dimensions={1} | all-to-all | bytes 393216 | tf_op jit(solution)/shard_map/all_to_all | solution.py:640
  49.8 0.7 %convert_reduce_fusion = f32[3,32,256]{2,1,0:T(8,128)} fusion(bf16[3,4,32,256]{3,2,0,1:T(8,128)(2,1)S(1)} %all_to_all.5), kind=kLoop, calls=%fused_computation | loop fusion | flops 172032 | bytes 294912 | tf_op jit(solution)/shard_map/reduce_sum | solution.py:641
  (4 shorter events, 0.1 us)
Async XLA Ops:
  0.1 1.1 %copy-start.4 = (bf16[64,2,3072]{2,1,0:T(2,128)(2,1)S(1)}, bf16[64,2,3072]{2,1,0:T(2,128)(2,1)}, u32[]{:S(2)}) copy-start(bf16[64,2,3072]{2,1,0:T(2,128)(2,1)} %param.5) | copy-start | bytes 2359300
  1.3 0.7 %copy-start = (s32[2,512]{1,0:T(2,128)S(1)}, s32[2,512]{1,0:T(2,128)}, u32[]{:S(2)}) copy-start(s32[2,512]{1,0:T(2,128)} %off_smem.1) | copy-start | bytes 12292
  1.3 0.7 %copy-start.1 = (f32[16,48]{1,0:T(8,128)S(1)}, f32[16,48]{1,0:T(8,128)}, u32[]{:S(2)}) copy-start(f32[16,48]{1,0:T(8,128)} %coef_ref.1) | copy-start | bytes 9220
  2.0 26.9 %copy-start.2 = (s32[3,2,136]{2,1,0:T(2,128)S(1)}, s32[3,2,136]{2,1,0:T(2,128)}, u32[]{:S(2)}) copy-start(s32[3,2,136]{2,1,0:T(2,128)} %cells_ref.1) | copy-start | bytes 9796
  2.0 26.9 %copy-start.3 = (f32[8,7]{1,0:T(8,128)S(1)}, f32[8,7]{1,0:T(8,128)}, u32[]{:S(2)}) copy-start(f32[8,7]{1,0:T(8,128)} %table_ref.1) | copy-start | bytes 676
where the time goes:
time: 50.7 us; the launch traced here: 50.4 us
  Pallas kernels  39.8 us (79%)
  blocking collectives  7.96 us (16%)
  local copies, waits for them, and re-layouts  1.87 us (4%)
  other arithmetic  0.75 us (1%)
    pallas_call x1, Pallas kernels, kernel_body(): pl.pallas_call(functools.partial(front_kernel, dims), out_shape=[jax.Shap...  26.9 us
    pallas_call x1, Pallas kernels, kernel_body(): pl.pallas_call(functools.partial(back_kernel, dims), out_shape=jax.ShapeD...  12.9 us
    all_to_all x1, blocking collectives, kernel_body(): lax.all_to_all(planes, 'grid', split_axis=1, concat_axis=1, tiled=True)  7.96 us
    unnamed x10, local copies, waits for them, and re-layouts  1.04 us

commit v1 on v0

--- a/solution.py
+++ b/solution.py
@@ -237,10 +237,12 @@
     return sorted(range(1, n), key=lambda k: abs(2 * k - n))
 
 
-def front_kernel(
-    dims, v_ref, coef_ref, tw_ref, off_ref, off_smem, recv_ref, drecv_ref,
-    vext, wide, spec, send, own, vis, left, picks, dsend,
+def whole_kernel(
+    dims, v_ref, coef_ref, tw_ref, off_ref, cells_ref, off_smem, table_ref, out_ref,
+    vext, wide, spec, send, own, vis, left, picks, dsend, recv_ref, drecv_ref,
+    perm, bands, vweights, oweights, cols, xs, sums, placed, rs_send, rs_recv,
     in_sem, halo_send, halo_recv, send_sem, recv_sem, dsend_sem, drecv_sem,
+    rs_send_sem, rs_recv_sem,
 ):
     n_stn, n_grid, chans, taps, frame_len, st = dims
     me, here = lax.axis_index("stn"), lax.axis_index("grid")
@@ -272,8 +274,12 @@
     shifted_line = jnp.concatenate(
         [line if f == 0 else pltpu.roll(line, f * frame_len, 1) for f in range(STEP)], axis=0
     )
-    for r in range(2 * n_stn * chans):
-        wide[r * STEP : (r + 1) * STEP, :] = (tw_ref[r : r + 1, :] * shifted_line).astype(bf16)
+
+    def build(c):
+        for r in range(2 * n_stn * c, 2 * n_stn * (c + 1)):
+            wide[r * STEP : (r + 1) * STEP, :] = (tw_ref[r : r + 1, :] * shifted_line).astype(bf16)
+
+    build(0)
 
     offs = off_ref[...].astype(f32)
     stations = offs.shape[1]
@@ -332,29 +338,42 @@
     def _():
         vext[:, 0:halo] = jnp.zeros((LANES, halo), bf16)
 
-    copies = []
+    copies, arrivals = [], []
+
+    def summed(c, k):
+        to = lax.rem(me + k, n_stn)
+        got = dot_nt(gather_rows, spec[c, to].reshape(LANES, LANES))
+        alone = got[ROWS:].astype(bf16)
+        own[c, to] = jnp.concatenate([alone[:st], alone[st:]], axis=1)
+        send[c, to] = got[:ROWS].astype(bf16)
+        if not k:
+            recv_ref[c, me] = send[c, me]
+
+    def sent(c, k):
+        to = lax.rem(me + k, n_stn)
+        copy = pltpu.make_async_remote_copy(
+            src_ref=send.at[c, to],
+            dst_ref=recv_ref.at[c, me],
+            send_sem=send_sem.at[c, k],
+            recv_sem=recv_sem.at[c, k],
+            device_id=(to, here),
+            device_id_type=MESH,
+        )
+        copy.start()
+        copies.append(copy)
+        arrivals[c].append(copy)
+
     for c in range(chans):
+        if c:
+            build(c)
         for t in range(blocks) if c else (0,):
             filtered(c, t)
-        for k in order + [0]:
-            to = lax.rem(me + k, n_stn)
-            got = dot_nt(gather_rows, spec[c, to].reshape(LANES, LANES))
-            send[c, to] = got[:ROWS].astype(bf16)
-            alone = got[ROWS:].astype(bf16)
-            own[c, to] = jnp.concatenate([alone[:st], alone[st:]], axis=1)
-            if k:
-                copy = pltpu.make_async_remote_copy(
-                    src_ref=send.at[c, to],
-                    dst_ref=recv_ref.at[c, me],
-                    send_sem=send_sem.at[c, k],
-                    recv_sem=recv_sem.at[c, k],
-                    device_id=(to, here),
-                    device_id_type=MESH,
-                )
-                copy.start()
-                copies.append(copy)
-            else:
-                recv_ref[c, me] = send[c, me]
+        arrivals.append([])
+        for k in order:
+            summed(c, k)
+            if c < chans - 1:
+                sent(c, k)
+        summed(c, 0)
 
     vis[...] = jnp.zeros(vis.shape, f32)
     lane2 = iota((st, 2 * LANES), 1)
@@ -397,8 +416,15 @@
             picks[first : first + TILE, a * LANES : (a + 1) * LANES] = hit
             picks[first : first + TILE, (1 - a) * LANES : (2 - a) * LANES] = blank
     binned = dot(left[...], picks[...])
-    binned = (binned[:half] + binned[half:]).reshape(n_stn, 8, 2 * LANES)
-    dsend[...] = binned
+    binned = binned[:half] + binned[half:]
+    dsend[...] = jnp.concatenate(
+        [
+            binned[:, a * LANES : (a + 1) * LANES].reshape(n_stn, 8, LANES)
+            for a in range(2)
+        ],
+        axis=1,
+    ).astype(bf16)
+    own_arrivals = []
     for k in order:
         to = lax.rem(me + k, n_stn)
         copy = pltpu.make_async_remote_copy(
@@ -411,29 +437,18 @@
         )
         copy.start()
         copies.append(copy)
+        own_arrivals.append(copy)
     drecv_ref[me] = dsend[me]
-
-    for copy in copies:
-        copy.wait()
-
-    @pl.when(here < n_grid - 1)
-    def _():
-        halo_copy.wait_send()
-
-
-def back_kernel(
-    dims, recv_ref, drecv_ref, cells_ref, table_ref, out_ref,
-    perm, bands, vweights, xs, sums, placed,
-):
-    n_stn, n_grid, chans, taps, frame_len, st = dims
-    me = lax.axis_index("stn")
+    for k in order:
+        sent(chans - 1, k)
+
     tiles = 2 * n_stn
     over, kern = table_ref.shape
     divisor = frame_len - 1
     side = SPREAD * tiles
     full = SPREAD * side
     depth = 2 * LANES
-    wide = tiles * PATCH
+    across_w = tiles * PATCH
 
     shape = (perm.shape[1], perm.shape[2])
     r, col = iota(shape, 0), iota(shape, 1)
@@ -470,14 +485,14 @@
     placed[...] = jnp.zeros(placed.shape, bf16)
     norm = 1.0 / (n_grid * depth // 2)
     rows_t = (16, UV)
-    rows_w = (16, wide)
-    same_tile = iota((tiles, wide), 0) == iota((tiles, wide), 1) // PATCH
+    rows_w = (16, across_w)
+    same_tile = iota((tiles, across_w), 0) == iota((tiles, across_w), 1) // PATCH
     own_lane = iota((32, LANES), 1) // SEPS
     lane_p = (2 * tiles, LANES)
     for c in range(chans):
         cells = cells_ref[c].astype(f32)
         row_line = dot(jnp.broadcast_to(cells[0:1], (16, npair)).astype(bf16), choose)[0:1] + absent
-        col_rows = dot_nt(choose_t, jnp.broadcast_to(cells[1:2], (LANES, npair)).astype(bf16))
+        cols[c] = dot_nt(choose_t, jnp.broadcast_to(cells[1:2], (LANES, npair)).astype(bf16))
         spot = iota((UV, PAIR_ROWS), 0).astype(f32) == row_line
         spots = ones_where(spot)
         lines = weight_rows(c, iota(rows_t, 0), (UV - iota(rows_t, 1)) % UV)
@@ -493,13 +508,22 @@
                 at = q - s + SPREAD - 1
                 part = jnp.where(same_tile, across[at : at + 1], 0.0)
                 top, low = split(part)
-                vweights[0, s, q * tiles : (q + 1) * tiles, :] = top
-                vweights[1, s, q * tiles : (q + 1) * tiles, :] = low
-            vweights[0, s, side:, :] = jnp.zeros((LANES - side, wide), bf16)
-            vweights[1, s, side:, :] = jnp.zeros((LANES - side, wide), bf16)
+                vweights[c, 0, s, q * tiles : (q + 1) * tiles, :] = top
+                vweights[c, 1, s, q * tiles : (q + 1) * tiles, :] = low
+            vweights[c, 0, s, side:, :] = jnp.zeros((LANES - side, across_w), bf16)
+            vweights[c, 1, s, side:, :] = jnp.zeros((LANES - side, across_w), bf16)
         onto = ones_where(iota((LANES, 16), 0) % SEPS == iota((LANES, 16), 1))
         a_top, a_low = split(across)
-        own_top, own_low = dot(onto, a_top).astype(bf16), dot(onto, a_low).astype(bf16)
+        oweights[c, 0] = dot(onto, a_top).astype(bf16)
+        oweights[c, 1] = dot(onto, a_low).astype(bf16)
+
+    reduced = []
+    for c in range(chans):
+        for copy in arrivals[c]:
+            copy.wait_recv()
+        if c == 0:
+            for copy in own_arrivals:
+                copy.wait_recv()
 
         got = recv_ref[c].reshape(n_stn * ROWS, LANES)
         lane_h = iota((full, LANES), 1) < LANES // 2
@@ -524,32 +548,32 @@
                 for s in range(SPREAD):
                     sums[0, s, at : at + tiles, :] = top[s * tiles : (s + 1) * tiles]
                     sums[1, s, at : at + tiles, :] = low[s * tiles : (s + 1) * tiles]
-        patches = jnp.zeros((2 * SEPS * tiles, wide), f32)
+        patches = jnp.zeros((2 * SEPS * tiles, across_w), f32)
         for s in range(SPREAD):
             for i, j in ((0, 0), (1, 0), (0, 1)):
-                patches = patches + dot(sums[i, s], vweights[j, s])
-
-        rr, cc = iota((32, n_stn * 8), 0), iota((32, n_stn * 8), 1)
-        take = ones_where(cc == (rr % tiles // 2) * 8 + c * 2 + rr // tiles)
-        d_top, d_low = split(drecv_ref[...].reshape(n_stn * 8, 2 * LANES))
-        own = dot(take, d_top) + dot(take, d_low)
-        odd = iota((32, LANES), 0) % 2 == 1
-        own = jnp.where(odd, own[:, LANES:], own[:, :LANES])
+                patches = patches + dot(sums[i, s], vweights[c, j, s])
+
+        rr, cc = iota((32, n_stn * 16), 0), iota((32, n_stn * 16), 1)
+        b = rr % tiles
+        take = ones_where(cc == (b // 2) * 16 + (b % 2) * 8 + c * 2 + rr // tiles)
+        mine = dot(take, drecv_ref[...].reshape(n_stn * 16, LANES))
         own_parts = []
         for e in range(2):
             for du in range(SEPS):
                 own_parts.append(
-                    jnp.where(own_lane == du, own, 0.0)[e * tiles : (e + 1) * tiles]
+                    jnp.where(own_lane == du, mine, 0.0)[e * tiles : (e + 1) * tiles]
                 )
         own_all = jnp.concatenate(own_parts, axis=0)
         o_top, o_low = split(own_all)
-        own_patch = dot(o_top, own_top) + dot(o_low, own_top) + dot(o_top, own_low)
+        own_patch = (
+            dot(o_top, oweights[c, 0]) + dot(o_low, oweights[c, 0]) + dot(o_top, oweights[c, 1])
+        )
         rr, cc = iota(patches.shape, 0), iota(patches.shape, 1)
         patches = jnp.where(rr % tiles == cc // PATCH, own_patch, patches)
 
         for a in range(tiles):
             low_rows = 8 if a >= 8 else 0
-            distance = iota((tiles, LANES), 1) - col_rows[a * tiles : (a + 1) * tiles].astype(i32)
+            distance = iota((tiles, LANES), 1) - cols[c, a * tiles : (a + 1) * tiles].astype(i32)
             distance = distance[low_rows:]
             valid = (distance >= 0) & (distance < PATCH)
             index = jnp.where(valid, distance + (a % 8) * PATCH, 0)
@@ -569,7 +593,32 @@
         for du in range(SEPS):
             plane = plane + dot(bands[c, du], placed[du])
         plane = (plane[:UV] + plane[UV:]) * norm
-        out_ref[c] = plane.astype(bf16)
+        rs_send[c] = plane.astype(bf16).reshape(n_grid, UV // n_grid, 2 * UV)
+        for k in range(1, n_grid):
+            to = lax.rem(here + k, n_grid)
+            copy = pltpu.make_async_remote_copy(
+                src_ref=rs_send.at[c, to],
+                dst_ref=rs_recv.at[c, k],
+                send_sem=rs_send_sem.at[c, k],
+                recv_sem=rs_recv_sem.at[c, k],
+                device_id=(me, to),
+                device_id_type=MESH,
+            )
+            copy.start()
+            reduced.append(copy)
+
+    for c in range(chans):
+        total = rs_send[c, here].astype(f32)
+        for k in range(1, n_grid):
+            reduced[c * (n_grid - 1) + k - 1].wait_recv()
+            total = total + rs_recv[c, k].astype(f32)
+        out_ref[c] = total
+    for copy in copies + reduced:
+        copy.wait_send()
+
+    @pl.when(here < n_grid - 1)
+    def _():
+        halo_copy.wait_send()
 
 
 def kernel_body(voltages, pfb_coeffs, station_offsets, tile_cells, kernel_table):
@@ -588,14 +637,14 @@
     smem = pl.BlockSpec(memory_space=pltpu.SMEM)
     anywhere = pl.BlockSpec(memory_space=pl.ANY)
     flat = voltages.reshape(st * pols, samples)
-    recv, drecv = pl.pallas_call(
-        functools.partial(front_kernel, dims),
-        out_shape=[
-            jax.ShapeDtypeStruct((chans, n_stn, ROWS, LANES), bf16),
-            jax.ShapeDtypeStruct((n_stn, 8, 2 * LANES), f32),
-        ],
-        in_specs=[anywhere, vmem, vmem, vmem, smem],
-        out_specs=[vmem, vmem],
+    tiles = 2 * n_stn
+    full = SPREAD * SPREAD * tiles
+    strip = UV // n_grid
+    summed = pl.pallas_call(
+        functools.partial(whole_kernel, dims),
+        out_shape=jax.ShapeDtypeStruct((chans, strip, 2 * UV), f32),
+        in_specs=[anywhere, vmem, vmem, vmem, vmem, smem, smem],
+        out_specs=vmem,
         scratch_shapes=[
             pltpu.VMEM((LANES, taps * frame_len + samples), bf16),
             pltpu.VMEM((2 * n_stn * chans * STEP, reach), bf16),
@@ -605,7 +654,19 @@
             pltpu.VMEM((n_stn * 8, st, LANES), f32),
             pltpu.VMEM((n_stn * 16, TILE * st), bf16),
             pltpu.VMEM((TILE * st, 2 * LANES), bf16),
-            pltpu.VMEM((n_stn, 8, 2 * LANES), f32),
+            pltpu.VMEM((n_stn, 16, LANES), bf16),
+            pltpu.VMEM((chans, n_stn, ROWS, LANES), bf16),
+            pltpu.VMEM((n_stn, 16, LANES), bf16),
+            pltpu.VMEM((2, full + 48, n_stn * ROWS), bf16),
+            pltpu.VMEM((chans, SEPS, 2 * UV, PAIR_ROWS), bf16),
+            pltpu.VMEM((chans, 2, SPREAD, LANES, tiles * PATCH), bf16),
+            pltpu.VMEM((chans, 2, LANES, tiles * PATCH), bf16),
+            pltpu.VMEM((chans, PAIR_ROWS, LANES), f32),
+            pltpu.VMEM((full + 48, 2 * LANES), bf16),
+            pltpu.VMEM((2, SPREAD, 2 * SEPS * tiles, LANES), bf16),
+            pltpu.VMEM((SEPS, PAIR_ROWS, 2 * UV), bf16),
+            pltpu.VMEM((chans, n_grid, strip, 2 * UV), bf16),
+            pltpu.VMEM((chans, n_grid, strip, 2 * UV), bf16),
             pltpu.SemaphoreType.DMA,
             pltpu.SemaphoreType.DMA,
             pltpu.SemaphoreType.DMA,
@@ -613,32 +674,14 @@
             pltpu.SemaphoreType.DMA((chans, n_stn)),
             pltpu.SemaphoreType.DMA((n_stn,)),
             pltpu.SemaphoreType.DMA((n_stn,)),
+            pltpu.SemaphoreType.DMA((chans, n_grid)),
+            pltpu.SemaphoreType.DMA((chans, n_grid)),
         ],
         compiler_params=pltpu.CompilerParams(
             collective_id=0, has_side_effects=True, vmem_limit_bytes=48 << 20
         ),
-    )(flat, pfb_coeffs, table, station_offsets, station_offsets)
-
-    tiles = 2 * n_stn
-    full = SPREAD * SPREAD * tiles
-    planes = pl.pallas_call(
-        functools.partial(back_kernel, dims),
-        out_shape=jax.ShapeDtypeStruct((chans, UV, 2 * UV), bf16),
-        in_specs=[vmem, vmem, vmem, smem],
-        out_specs=vmem,
-        scratch_shapes=[
-            pltpu.VMEM((2, full + 48, n_stn * ROWS), bf16),
-            pltpu.VMEM((chans, SEPS, 2 * UV, PAIR_ROWS), bf16),
-            pltpu.VMEM((2, SPREAD, LANES, tiles * PATCH), bf16),
-            pltpu.VMEM((full + 48, 2 * LANES), bf16),
-            pltpu.VMEM((2, SPREAD, 2 * SEPS * tiles, LANES), bf16),
-            pltpu.VMEM((SEPS, PAIR_ROWS, 2 * UV), bf16),
-        ],
-        compiler_params=pltpu.CompilerParams(vmem_limit_bytes=48 << 20),
-    )(recv, drecv, tile_cells, kernel_table)
-    planes = planes.reshape(chans, n_grid, UV // n_grid, 2 * UV)
-    parts = lax.all_to_all(planes, "grid", split_axis=1, concat_axis=1, tiled=True)
-    return jnp.transpose(parts.astype(f32).sum(axis=1), (1, 0, 2))
+    )(flat, pfb_coeffs, table, station_offsets, tile_cells, station_offsets, kernel_table)
+    return jnp.transpose(summed, (1, 0, 2))
 
 
 def kernels_fit(mesh, args):

time: 50.7 us -> 41.8 us (0.82)
  blocking collectives: 7.96 us -> 0 us
  Pallas kernels: 39.8 us -> 38.9 us
  other arithmetic: 0.75 us -> 0.08 us
  local copies, waits for them, and re-layouts: 1.87 us -> 2.51 us
    all_to_all x1 -> x0, blocking collectives: 7.96 us -> none  [kernel_body(): lax.all_to_all(planes, 'grid', split_axis=1, concat_axis=1, tiled=True)]
    pallas_call x2 -> x1, Pallas kernels: 39.8 us -> 38.9 us  [kernel_body(): pl.pallas_call(functools.partial(whole_kernel, dims), out_shape=jax.Shape...]
    reduce_sum x1 -> x0, other arithmetic: 0.67 us -> none  [kernel_body(): return jnp.transpose(parts.astype(f32).sum(axis=1), (1, 0, 2))]
    unnamed x10 -> x11, local copies, waits for them, and re-layouts: 1.04 us -> 1.69 us
where the time goes in v1:
time: 41.8 us; the launch traced here: 41.6 us
  Pallas kernels  38.9 us (93%)
  local copies, waits for them, and re-layouts  2.51 us (6%)
    pallas_call x1, Pallas kernels, kernel_body(): pl.pallas_call(functools.partial(whole_kernel, dims), out_shape=jax.Shape...  38.9 us
    unnamed x11, local copies, waits for them, and re-layouts  1.69 us

profile of v1, /device:TPU:0, one launch (start us, length us, event | category | flops | bytes accessed | tf_op | source)
XLA Modules:
  0.0 41.6 jit_solution(5926081175033463600)
XLA Ops:
  0.0 0.1 multiply_convert_fusion
  0.1 0.0 copy-start.4
  0.1 0.1 tile.14
  0.2 0.4 %tile.15.tw_ref = f32[48,1536]{1,0:T(8,128)S(1)} reshape(f32[48,32,48]{2,1,0:T(8,128)S(1)} %tile.14) | data formatting | bytes 589824 | tf_op jit(solution)/shard_map/tile | solution.py:635
  0.7 0.6 %copy-done.4 = bf16[64,2,3072]{2,1,0:T(2,128)(2,1)S(1)} copy-done((bf16[64,2,3072]{2,1,0:T(2,128)(2,1)S(1)}, bf16[64,2,3072]{2,1,0:T(2,128)(2,1)}, u32[]{:S(2)}) %copy-start.4) | copy-done | bytes 786456
  1.3 0.0 copy-start
  1.3 0.0 copy-start.1
  1.3 0.0 copy-start.2
  1.3 0.0 copy-start.3
  1.3 0.3 reshape.78.v_ref
  1.6 0.4 copy-done
  2.0 0.0 copy-done.1
  2.0 0.0 copy-done.2
  2.0 0.0 copy-done.3
  2.0 38.9 %shard_map.55 = f32[3,32,256]{2,1,0:T(8,128)S(1)} custom-call(bf16[128,3072]{1,0:T(8,128)(2,1)S(1)} %reshape.78.v_ref, f32[16,48]{1,0:T(8,128)S(1)} %copy-done.1, f32[48,1536]{1,0:T(8,128)S(1)} %tile.15.tw_ref, s32[2,512]{1,0:T(2,128)S(1)} %copy-done, s32[3,2,136]{2,1,0:T(2,128)S(1)} %copy-done.2, s32[2,512]{1,0:T(2,128)S(1)} %copy-done, f32[8,7]{1,0:T(8,128)S(1)} %copy-done.3), custom_call_target="tpu_custom_call" | custom-call | tf_op jit(solution)/shard_map/pallas_call | solution.py:643
  40.9 0.6 %copy.10 = f32[32,3,256]{2,0,1:T(8,128)} copy(f32[32,3,256]{2,0,1:T(8,128)S(1)} %bitcast.9) | data formatting | bytes 196608
  (3 shorter events, 0.0 us)
Async XLA Ops:
  0.1 1.1 %copy-start.4 = (bf16[64,2,3072]{2,1,0:T(2,128)(2,1)S(1)}, bf16[64,2,3072]{2,1,0:T(2,128)(2,1)}, u32[]{:S(2)}) copy-start(bf16[64,2,3072]{2,1,0:T(2,128)(2,1)} %param.5) | copy-start | bytes 2359300
  1.3 0.7 %copy-start = (s32[2,512]{1,0:T(2,128)S(1)}, s32[2,512]{1,0:T(2,128)}, u32[]{:S(2)}) copy-start(s32[2,512]{1,0:T(2,128)} %off_smem.1) | copy-start | bytes 12292
  1.3 0.7 %copy-start.1 = (f32[16,48]{1,0:T(8,128)S(1)}, f32[16,48]{1,0:T(8,128)}, u32[]{:S(2)}) copy-start(f32[16,48]{1,0:T(8,128)} %coef_ref.1) | copy-start | bytes 9220
  1.3 0.7 %copy-start.2 = (s32[3,2,136]{2,1,0:T(2,128)S(1)}, s32[3,2,136]{2,1,0:T(2,128)}, u32[]{:S(2)}) copy-start(s32[3,2,136]{2,1,0:T(2,128)} %cells_ref.1) | copy-start | bytes 9796
  1.3 0.7 %copy-start.3 = (f32[8,7]{1,0:T(8,128)S(1)}, f32[8,7]{1,0:T(8,128)}, u32[]{:S(2)}) copy-start(f32[8,7]{1,0:T(8,128)} %table_ref.1) | copy-start | bytes 676

commit v2 on v1

--- a/solution.py
+++ b/solution.py
@@ -207,8 +207,8 @@
 MESH = pl.DeviceIdType.MESH
 SEPS = 2 * SPREAD - 1
 STEP = 16
-ROWS = 112
 LANES = 128
+SUMS = 2 * CLASSES
 PAIR_ROWS = 256
 
 
@@ -237,19 +237,30 @@
     return sorted(range(1, n), key=lambda k: abs(2 * k - n))
 
 
+def padded(rows):
+    return -(-rows // 16) * 16
+
+
+def channels_of(start, stop):
+    return range(start // SUMS, (stop - 1) // SUMS + 1)
+
+
 def whole_kernel(
-    dims, v_ref, coef_ref, tw_ref, off_ref, cells_ref, off_smem, table_ref, out_ref,
-    vext, wide, spec, send, own, vis, left, picks, dsend, recv_ref, drecv_ref,
-    perm, bands, vweights, oweights, cols, xs, sums, placed, rs_send, rs_recv,
-    in_sem, halo_send, halo_recv, send_sem, recv_sem, dsend_sem, drecv_sem,
-    rs_send_sem, rs_recv_sem,
+    dims, groups, v_ref, coef_ref, tw_ref, off_ref, cells_ref, table_ref, out_ref,
+    vext, wide, spec, own, vis, left, picks, dsend, drecv_ref,
+    bands, vweights, oweights, cols, xs, sums, placed, rs_send, rs_recv, *rest
 ):
     n_stn, n_grid, chans, taps, frame_len, st = dims
+    n_msg = len(groups)
+    sends, recvs, flats = rest[:n_msg], rest[n_msg : 2 * n_msg], rest[2 * n_msg : 3 * n_msg]
+    (
+        in_sem, halo_send, halo_recv, send_sem, recv_sem, dsend_sem, drecv_sem,
+        rs_send_sem, rs_recv_sem,
+    ) = rest[3 * n_msg :]
     me, here = lax.axis_index("stn"), lax.axis_index("grid")
     reach = (STEP + taps) * frame_len
     halo = taps * frame_len
     samples = v_ref.shape[1]
-    blocks = samples // (STEP * frame_len)
     order = send_order(n_stn)
 
     barrier = pltpu.get_barrier_semaphore()
@@ -274,8 +285,10 @@
     shifted_line = jnp.concatenate(
         [line if f == 0 else pltpu.roll(line, f * frame_len, 1) for f in range(STEP)], axis=0
     )
+    built = set()
 
     def build(c):
+        built.add(c)
         for r in range(2 * n_stn * c, 2 * n_stn * (c + 1)):
             wide[r * STEP : (r + 1) * STEP, :] = (tw_ref[r : r + 1, :] * shifted_line).astype(bf16)
 
@@ -288,14 +301,18 @@
     row_of = (stations, LANES)
     mine = ones_where(iota(row_of, 0) == me * st + iota(row_of, 1) // 2)
     cls_line = dot(cls, mine)[0:1]
+    kap_line = dot(kap[:16], mine)[0:1]
     lane = iota((1, LANES), 1)
-    code = ((lane % 2) * 2 + lane // 2 // TILE).astype(f32) * CLASSES + cls_line
-    line_a = iota((ROWS, LANES), 0).astype(f32)
-    sum_rows = ones_where(line_a == code)
-    line_b = iota((LANES, LANES), 0)
-    lane_b = iota((LANES, LANES), 1)
-    own_rows = ones_where(line_b == (lane_b % 2) * st + lane_b // 2)
-    gather_rows = jnp.concatenate([sum_rows, own_rows], axis=0)
+    code = (lane // 2 // TILE).astype(f32) * CLASSES + cls_line
+
+    def class_rows(start, stop):
+        lines = iota((padded(stop - start), LANES), 0)
+        lines = jnp.where(lines < stop - start, lines + start, -1).astype(f32)
+        return jnp.concatenate(
+            [ones_where(lines == code + c * SUMS) for c in channels_of(start, stop)], axis=1
+        )
+
+    own_rows = ones_where(iota((st, LANES), 0) == iota((st, LANES), 1) // 2)
 
     pl.semaphore_wait(barrier, n_stn + n_grid - 2)
 
@@ -311,15 +328,76 @@
         ).start()
 
     load.wait()
-
-    def filtered(c, t):
+    even = iota((2 * n_stn * STEP, LANES), 1) % 2 == 0
+
+    def filtered(h, c):
         rows = wide[c * 2 * n_stn * STEP : (c + 1) * 2 * n_stn * STEP, :]
-        window = vext[:, t * STEP * frame_len : t * STEP * frame_len + reach]
-        got = dot_nt(rows, window).astype(bf16)
-        spec[c, :, :, t] = got.reshape(n_stn, 2, STEP, LANES)
-
-    for t in range(1, blocks):
-        filtered(0, t)
+        first = 2 * h * STEP * frame_len
+        second = first + STEP * frame_len
+        window = jnp.concatenate(
+            [vext[:, first : first + reach], vext[:, second : second + reach]], axis=0
+        )
+        got = dot_nt(rows, window)
+        for t in range(2):
+            part = got[:, t * LANES : (t + 1) * LANES]
+            for p in range(2):
+                only = jnp.where(even if p == 0 else ~even, part, 0.0).astype(bf16)
+                spec[h, :, :, p, t, :, c * LANES : (c + 1) * LANES] = only.reshape(
+                    n_stn, 2, STEP, LANES
+                )
+
+    copies, arrivals = [], [[] for _ in groups]
+
+    passed = set()
+
+    def made(m, send_now):
+        h, start, stop = groups[m]
+        for c in channels_of(start, stop):
+            if c not in built:
+                build(c)
+            if (h, c) not in passed:
+                passed.add((h, c))
+                filtered(h, c)
+        cs = channels_of(start, stop)
+        pick_rows = class_rows(start, stop)
+        for k in order + [0]:
+            to = lax.rem(me + k, n_stn)
+            block = spec[h, to, :, :, :, :, cs[0] * LANES : (cs[-1] + 1) * LANES]
+            got = dot_nt(pick_rows, block.reshape(LANES, len(cs) * LANES)).astype(bf16)
+            sends[m][to] = got
+            if k and send_now:
+                sent(m, k)
+        recvs[m][me] = sends[m][me]
+
+    def sent(m, k):
+        to = lax.rem(me + k, n_stn)
+        copy = pltpu.make_async_remote_copy(
+            src_ref=sends[m].at[to],
+            dst_ref=recvs[m].at[me],
+            send_sem=send_sem.at[m, k],
+            recv_sem=recv_sem.at[m, k],
+            device_id=(to, here),
+            device_id_type=MESH,
+        )
+        copy.start()
+        copies.append(copy)
+        arrivals[m].append(copy)
+
+    def kept(h):
+        for c in range(chans):
+            for d in range(0, n_stn, 2):
+                block = spec[h, d : d + 2, :, :, :, :, c * LANES : (c + 1) * LANES]
+                got = dot_nt(own_rows, block.reshape(2 * LANES, LANES)).astype(bf16)
+                for j in range(2):
+                    own[c, d + j, :, h * LANES : (h + 1) * LANES] = got[
+                        :, j * LANES : (j + 1) * LANES
+                    ]
+
+    early = [m for m, group in enumerate(groups) if group[0] == 1]
+    late = [m for m, group in enumerate(groups) if group[0] == 0]
+    for m in early:
+        made(m, True)
+    kept(1)
 
     halo_copy = pltpu.make_async_remote_copy(
         src_ref=v_ref.at[:, pl.ds(samples - halo, halo)],
@@ -338,46 +416,16 @@
     def _():
         vext[:, 0:halo] = jnp.zeros((LANES, halo), bf16)
 
-    copies, arrivals = [], []
-
-    def summed(c, k):
-        to = lax.rem(me + k, n_stn)
-        got = dot_nt(gather_rows, spec[c, to].reshape(LANES, LANES))
-        alone = got[ROWS:].astype(bf16)
-        own[c, to] = jnp.concatenate([alone[:st], alone[st:]], axis=1)
-        send[c, to] = got[:ROWS].astype(bf16)
-        if not k:
-            recv_ref[c, me] = send[c, me]
-
-    def sent(c, k):
-        to = lax.rem(me + k, n_stn)
-        copy = pltpu.make_async_remote_copy(
-            src_ref=send.at[c, to],
-            dst_ref=recv_ref.at[c, me],
-            send_sem=send_sem.at[c, k],
-            recv_sem=recv_sem.at[c, k],
-            device_id=(to, here),
-            device_id_type=MESH,
-        )
-        copy.start()
-        copies.append(copy)
-        arrivals[c].append(copy)
-
-    for c in range(chans):
-        if c:
-            build(c)
-        for t in range(blocks) if c else (0,):
-            filtered(c, t)
-        arrivals.append([])
-        for k in order:
-            summed(c, k)
-            if c < chans - 1:
-                sent(c, k)
-        summed(c, 0)
-
-    vis[...] = jnp.zeros(vis.shape, f32)
+    for m in late:
+        made(m, m == late[0])
+    kept(0)
+
+    half = n_stn * 8
     lane2 = iota((st, 2 * LANES), 1)
     flip = jnp.where(lane2 % LANES < LANES // 2, 1.0, -1.0)
+    for c in range(chans, 4):
+        for d in range(n_stn):
+            vis[d * 8 + c * 2 : d * 8 + c * 2 + 2] = jnp.zeros((2, st, LANES), f32)
     for c in range(chans):
         for d in range(n_stn):
             x = own[c, d]
@@ -393,30 +441,25 @@
             got = dot_nt(both, jnp.concatenate([x, x], axis=0))
             for e in range(2):
                 vis[d * 8 + c * 2 + e] = got[e * st : (e + 1) * st]
-
-    half = n_stn * 8
     lane3 = iota((half, LANES), 1)
     for k in range(TILE // 2):
-        even = jnp.where(lane3 % st < TILE, vis[:, 2 * k, :], vis[:, 2 * k + TILE, :])
-        odd = jnp.where(lane3 % st < TILE, vis[:, 2 * k + 1, :], vis[:, 2 * k + 1 + TILE, :])
-        top, low = split(jnp.where(lane3 < st, even, odd))
-        left[0:half, k * LANES : (k + 1) * LANES] = top
-        left[half:, k * LANES : (k + 1) * LANES] = low
+        first = jnp.where(lane3 % st < TILE, vis[:, 2 * k, :], vis[:, 2 * k + TILE, :])
+        second = jnp.where(lane3 % st < TILE, vis[:, 2 * k + 1, :], vis[:, 2 * k + 1 + TILE, :])
+        left[:, k * LANES : (k + 1) * LANES] = jnp.where(lane3 < st, first, second).astype(bf16)
     which = (st, stations)
     kap_col = dot_nt(ones_where(iota(which, 1) == me * st + iota(which, 0)), kap)
-    base = kap_col.astype(i32) + iota((st, LANES), 1) - (SEPS * (SPREAD - 1) + SPREAD - 1)
+    base = kap_col + iota((st, LANES), 1).astype(f32) - (SEPS * (SPREAD - 1) + SPREAD - 1)
     blank = jnp.zeros((TILE, LANES), bf16)
     row_t = iota((TILE, LANES), 0)
     for i in range(TILE):
         for a in range(2):
-            at = me * st + a * TILE + i
-            value = off_smem[0, at] * SEPS + off_smem[1, at]
+            at = 2 * (a * TILE + i)
+            value = kap_line[0:1, at : at + 1]
             hit = ones_where((base[a * TILE : (a + 1) * TILE] == value) & (row_t > i))
             first = i * st + a * TILE
             picks[first : first + TILE, a * LANES : (a + 1) * LANES] = hit
             picks[first : first + TILE, (1 - a) * LANES : (2 - a) * LANES] = blank
     binned = dot(left[...], picks[...])
-    binned = binned[:half] + binned[half:]
     dsend[...] = jnp.concatenate(
         [
             binned[:, a * LANES : (a + 1) * LANES].reshape(n_stn, 8, LANES)
@@ -440,7 +483,7 @@
         own_arrivals.append(copy)
     drecv_ref[me] = dsend[me]
     for k in order:
-        sent(chans - 1, k)
+        sent(late[1], k)
 
     tiles = 2 * n_stn
     over, kern = table_ref.shape
@@ -449,25 +492,20 @@
     full = SPREAD * side
     depth = 2 * LANES
     across_w = tiles * PATCH
-
-    shape = (perm.shape[1], perm.shape[2])
-    r, col = iota(shape, 0), iota(shape, 1)
-    b, q = r % tiles, r // tiles
-    for p in range(2):
-        want = (b // 2) * ROWS + (p * 2 + b % 2) * CLASSES + q
-        perm[p] = ones_where((col == want) & (r < full))
-
     npair = cells_ref.shape[2]
 
-    def pair_number(a, b):
-        return jnp.where(a <= b, a * tiles - a * (a - 1) // 2 + b - a, -1)
-
-    kl = (npair, PAIR_ROWS)
-    choose = ones_where(iota(kl, 0) == pair_number(iota(kl, 1) // tiles, iota(kl, 1) % tiles))
-    kr = (PAIR_ROWS, npair)
-    choose_t = ones_where(iota(kr, 1) == pair_number(iota(kr, 0) // tiles, iota(kr, 0) % tiles))
-    lane_pair = iota((1, PAIR_ROWS), 1)
-    absent = jnp.where(lane_pair // tiles <= lane_pair % tiles, 0.0, -1000.0)
+    def tile_of(x):
+        return 2 * (x % n_stn) + x // n_stn
+
+    def pair_number(x):
+        b = tile_of(x % tiles)
+        last = x // tiles == tiles - 1
+        a = jnp.where(last, b, tile_of(x // tiles))
+        return jnp.where((a < b) | last, a * tiles - a * (a - 1) // 2 + b - a, -1)
+
+    choose = ones_where(iota((npair, PAIR_ROWS), 0) == pair_number(iota((1, PAIR_ROWS), 1)))
+    choose_t = ones_where(iota((PAIR_ROWS, npair), 1) == pair_number(iota((PAIR_ROWS, 1), 0)))
+    absent = jnp.where(pair_number(iota((1, PAIR_ROWS), 1)) < 0, -1000.0, 0.0)
 
     def weight_rows(c, d, r):
         scaled = (d * (me * chans + c + frame_len // 2)).astype(f32)
@@ -482,60 +520,82 @@
                 got = jnp.where(code == o * kern + t, table_ref[o, t], got)
         return got
 
-    placed[...] = jnp.zeros(placed.shape, bf16)
+    xs[full:, :] = jnp.zeros((xs.shape[0] - full, depth), bf16)
     norm = 1.0 / (n_grid * depth // 2)
     rows_t = (16, UV)
     rows_w = (16, across_w)
     same_tile = iota((tiles, across_w), 0) == iota((tiles, across_w), 1) // PATCH
-    own_lane = iota((32, LANES), 1) // SEPS
-    lane_p = (2 * tiles, LANES)
+    own_block = iota((LANES, across_w), 0) // SEPS == iota((LANES, across_w), 1) // PATCH
+    onto = ones_where(iota((LANES, 16), 0) % SEPS == iota((LANES, 16), 1))
     for c in range(chans):
         cells = cells_ref[c].astype(f32)
         row_line = dot(jnp.broadcast_to(cells[0:1], (16, npair)).astype(bf16), choose)[0:1] + absent
         cols[c] = dot_nt(choose_t, jnp.broadcast_to(cells[1:2], (LANES, npair)).astype(bf16))
-        spot = iota((UV, PAIR_ROWS), 0).astype(f32) == row_line
-        spots = ones_where(spot)
+        spots = ones_where(iota((UV, PAIR_ROWS), 0).astype(f32) == row_line)
         lines = weight_rows(c, iota(rows_t, 0), (UV - iota(rows_t, 1)) % UV)
         for du in range(SEPS):
             band = pltpu.roll(
                 jnp.broadcast_to(lines[du : du + 1], (UV, UV)), 0, 1, stride=1, stride_axis=0
             )
             top, low = split(band)
-            bands[c, du] = dot(jnp.concatenate([top, low], axis=0), spots).astype(bf16)
+            bands[c, :, du * PAIR_ROWS : (du + 1) * PAIR_ROWS] = dot(
+                jnp.concatenate([top, low], axis=0), spots
+            ).astype(bf16)
         across = weight_rows(c, iota(rows_w, 0), iota(rows_w, 1) % PATCH)
-        for s in range(SPREAD):
-            for q in range(SPREAD):
-                at = q - s + SPREAD - 1
-                part = jnp.where(same_tile, across[at : at + 1], 0.0)
-                top, low = split(part)
-                vweights[c, 0, s, q * tiles : (q + 1) * tiles, :] = top
-                vweights[c, 1, s, q * tiles : (q + 1) * tiles, :] = low
-            vweights[c, 0, s, side:, :] = jnp.zeros((LANES - side, across_w), bf16)
-            vweights[c, 1, s, side:, :] = jnp.zeros((LANES - side, across_w), bf16)
-        onto = ones_where(iota((LANES, 16), 0) % SEPS == iota((LANES, 16), 1))
-        a_top, a_low = split(across)
-        oweights[c, 0] = dot(onto, a_top).astype(bf16)
-        oweights[c, 1] = dot(onto, a_low).astype(bf16)
-
+        for at in range(SEPS):
+            parts = split(jnp.where(same_tile, across[at : at + 1], 0.0))
+            for j in range(2):
+                vweights[c, j, at * tiles : (at + 1) * tiles, :] = parts[j]
+        for j in range(2):
+            vweights[c, j, SEPS * tiles :, :] = jnp.zeros((depth - SEPS * tiles, across_w), bf16)
+        for j, part in enumerate(split(across)):
+            oweights[c, j] = jnp.where(own_block, dot(onto, part), 0.0).astype(bf16)
+
+    for k in order:
+        sent(late[2], k)
+
+    ready = set()
     reduced = []
-    for c in range(chans):
-        for copy in arrivals[c]:
-            copy.wait_recv()
-        if c == 0:
-            for copy in own_arrivals:
-                copy.wait_recv()
-
-        got = recv_ref[c].reshape(n_stn * ROWS, LANES)
-        lane_h = iota((full, LANES), 1) < LANES // 2
+    lane_h = iota((tiles, LANES), 1) < LANES // 2
+    rows_p = 2 * SEPS * tiles
+    lane_s = iota((side, LANES), 1) < side
+    lane_p = iota((tiles, LANES), 1)
+
+    def found(h, g):
+        for m, (half, start, stop) in enumerate(groups):
+            if half == h and start <= g < stop:
+                if m not in ready:
+                    ready.add(m)
+                    for copy in arrivals[m]:
+                        copy.wait_recv()
+                    flats[m][...] = recvs[m][...].astype(f32)
+                return flats[m][:, g - start, :]
+
+    def moves(c, a):
+        distance = iota((tiles, LANES), 1) - cols[c, a * tiles : (a + 1) * tiles].astype(i32)
+        valid = (distance >= 0) & (distance < PATCH)
+        return valid, jnp.where(valid, distance, 0)
+
+    def correlated(c):
         turned = []
-        for p in range(2):
-            x = dot(perm[p], got)
-            xs[:, p * LANES : (p + 1) * LANES] = x.astype(bf16)
-            y = pltpu.roll(x[:full], LANES // 2, 1)
-            turned.append(jnp.where(lane_h, -y, y).astype(bf16))
-        lefts = [xs[:full], jnp.concatenate(turned, axis=1)]
+        for q in range(SPREAD * SPREAD):
+            pieces = []
+            for h in range(2):
+                x = jnp.concatenate(
+                    [found(h, c * SUMS + a * CLASSES + q) for a in range(2)], axis=0
+                )
+                xs[q * tiles : (q + 1) * tiles, h * LANES : (h + 1) * LANES] = x.astype(bf16)
+                y = pltpu.roll(x, LANES // 2, 1)
+                pieces.append(jnp.where(lane_h, -y, y).astype(bf16))
+            turned.append(jnp.concatenate(pieces, axis=1))
+        lefts = [xs[:full], jnp.concatenate(turned, axis=0)]
         for e in range(2):
-            blocks = [dot_nt(lefts[e], xs[q * side : q * side + LANES]) for q in range(SPREAD)]
+            blocks = []
+            for q in range(0, SPREAD, 2):
+                names = [r for r in (q, q + 1) if r < SPREAD]
+                rights = [xs[r * side : r * side + LANES] for r in names]
+                got = dot_nt(lefts[e], jnp.concatenate(rights, axis=0))
+                blocks += [got[:, j * LANES : (j + 1) * LANES] for j in range(len(names))]
             for du in range(SEPS):
                 d = du - (SPREAD - 1)
                 total = sum(
@@ -543,55 +603,54 @@
                     for s in range(SPREAD)
                     if 0 <= s + d < SPREAD
                 )
-                top, low = split(total)
+                total = jnp.where(lane_s, total, 0.0)
+                shifts = [
+                    pltpu.roll(
+                        total[x * tiles : (x + 1) * tiles], (SPREAD - 1 - x) * tiles, 1
+                    )
+                    for x in range(SPREAD - 1)
+                ]
+                wrap = (2 * SPREAD - 1) * tiles - LANES
+                main = total[(SPREAD - 1) * tiles :] + jnp.where(lane_p < wrap, 0.0, shifts[0])
+                for part in shifts[1:]:
+                    main = main + part
+                over_part = jnp.where(lane_p < wrap, shifts[0], 0.0)
+                top, low = split(jnp.concatenate([main, over_part], axis=1))
                 at = (e * SEPS + du) * tiles
-                for s in range(SPREAD):
-                    sums[0, s, at : at + tiles, :] = top[s * tiles : (s + 1) * tiles]
-                    sums[1, s, at : at + tiles, :] = low[s * tiles : (s + 1) * tiles]
-        patches = jnp.zeros((2 * SEPS * tiles, across_w), f32)
-        for s in range(SPREAD):
-            for i, j in ((0, 0), (1, 0), (0, 1)):
-                patches = patches + dot(sums[i, s], vweights[c, j, s])
-
-        rr, cc = iota((32, n_stn * 16), 0), iota((32, n_stn * 16), 1)
-        b = rr % tiles
-        take = ones_where(cc == (b // 2) * 16 + (b % 2) * 8 + c * 2 + rr // tiles)
-        mine = dot(take, drecv_ref[...].reshape(n_stn * 16, LANES))
-        own_parts = []
-        for e in range(2):
-            for du in range(SEPS):
-                own_parts.append(
-                    jnp.where(own_lane == du, mine, 0.0)[e * tiles : (e + 1) * tiles]
-                )
-        own_all = jnp.concatenate(own_parts, axis=0)
-        o_top, o_low = split(own_all)
-        own_patch = (
-            dot(o_top, oweights[c, 0]) + dot(o_low, oweights[c, 0]) + dot(o_top, oweights[c, 1])
-        )
-        rr, cc = iota(patches.shape, 0), iota(patches.shape, 1)
-        patches = jnp.where(rr % tiles == cc // PATCH, own_patch, patches)
-
-        for a in range(tiles):
-            low_rows = 8 if a >= 8 else 0
-            distance = iota((tiles, LANES), 1) - cols[c, a * tiles : (a + 1) * tiles].astype(i32)
-            distance = distance[low_rows:]
-            valid = (distance >= 0) & (distance < PATCH)
-            index = jnp.where(valid, distance + (a % 8) * PATCH, 0)
+                sums[at : at + tiles, :] = top
+                sums[rows_p + at : rows_p + at + tiles, :] = low
+        patches = dot(sums[...], vweights[c, 0])
+        patches = patches[:rows_p] + patches[rows_p:] + dot(sums[:rows_p], vweights[c, 1])
+
+        for a in range(tiles - 1):
+            valid, index = moves(c, a)
+            index = index + (a % 8) * PATCH
             for du in range(SEPS):
                 for e in range(2):
                     at = (e * SEPS + du) * tiles
-                    source = patches[
-                        at + low_rows : at + tiles, a // 8 * LANES : (a // 8 + 1) * LANES
-                    ]
+                    source = patches[at : at + tiles, a // 8 * LANES : (a // 8 + 1) * LANES]
                     moved = jnp.where(valid, jnp.take_along_axis(source, index, axis=1), 0.0)
-                    if low_rows:
-                        moved = jnp.concatenate([jnp.zeros((8, LANES), f32), moved], axis=0)
-                    placed[du, a * tiles : (a + 1) * tiles, e * LANES : (e + 1) * LANES] = (
-                        moved.astype(bf16)
+                    first = du * PAIR_ROWS + a * tiles
+                    placed[c, first : first + tiles, e * LANES : (e + 1) * LANES] = moved.astype(
+                        bf16
                     )
-        plane = jnp.zeros((2 * UV, 2 * UV), f32)
+
+    def gridded(c):
+        rr, cc = iota((32, n_stn * 16), 0), iota((32, n_stn * 16), 1)
+        b = rr % tiles
+        take = ones_where(cc == (b % n_stn) * 16 + (b // n_stn) * 8 + c * 2 + rr // tiles)
+        alone = dot(take, drecv_ref[...].reshape(n_stn * 16, LANES)).astype(bf16)
+        alone = dot(alone, oweights[c, 0]) + dot(alone, oweights[c, 1])
+        valid, index = moves(c, tiles - 1)
         for du in range(SEPS):
-            plane = plane + dot(bands[c, du], placed[du])
+            for e in range(2):
+                source = alone[e * tiles : (e + 1) * tiles, du // 8 * LANES : (du // 8 + 1) * LANES]
+                moved = jnp.take_along_axis(source, index + (du % 8) * PATCH, axis=1)
+                first = du * PAIR_ROWS + (tiles - 1) * tiles
+                placed[c, first : first + tiles, e * LANES : (e + 1) * LANES] = jnp.where(
+                    valid, moved, 0.0
+                ).astype(bf16)
+        plane = dot(bands[c], placed[c])
         plane = (plane[:UV] + plane[UV:]) * norm
         rs_send[c] = plane.astype(bf16).reshape(n_grid, UV // n_grid, 2 * UV)
         for k in range(1, n_grid):
@@ -607,6 +666,15 @@
             copy.start()
             reduced.append(copy)
 
+    for c in range(chans - 1):
+        correlated(c)
+    for copy in own_arrivals:
+        copy.wait_recv()
+    for c in range(chans - 1):
+        gridded(c)
+    correlated(chans - 1)
+    gridded(chans - 1)
+
     for c in range(chans):
         total = rs_send[c, here].astype(f32)
         for k in range(1, n_grid):
@@ -628,11 +696,20 @@
     chans = tile_cells.shape[0]
     dims = (n_stn, n_grid, chans, taps, frame_len, st)
     reach = (STEP + taps) * frame_len
-    blocks = samples // (STEP * frame_len)
-
-    table = dft_table(frame_len).astype(f32).T.reshape(n_stn, chans, 2, frame_len)
-    table = jnp.transpose(table, (1, 0, 2, 3)).reshape(-1, frame_len)
-    table = jnp.tile(table, (1, STEP + taps))
+    whole, first = chans * SUMS, padded(SUMS)
+    second = first + padded(2 * SUMS - first)
+    third = SUMS // 16 * 16
+    groups = (
+        (1, 0, third), (1, third, whole), (0, 0, first), (0, first, second), (0, second, whole),
+    )
+
+    line = np.arange(frame_len)[:, None] * np.arange(frame_len // 2)[None, :] % frame_len
+    angles = line.astype(np.float32) * np.float32(2.0 * math.pi / frame_len)
+    scale = np.float32(1.0 / math.sqrt(frame_len))
+    table = np.stack([np.cos(angles) * scale, -np.sin(angles) * scale], axis=2)
+    table = table.astype(jnp.bfloat16).astype(np.float32)
+    table = table.transpose(1, 2, 0).reshape(n_stn, chans, 2, frame_len).transpose(1, 0, 2, 3)
+    table = jnp.asarray(np.tile(table.reshape(-1, frame_len), (1, STEP + taps)))
     vmem = pl.BlockSpec(memory_space=pltpu.VMEM)
     smem = pl.BlockSpec(memory_space=pltpu.SMEM)
     anywhere = pl.BlockSpec(memory_space=pl.ANY)
@@ -640,38 +717,39 @@
     tiles = 2 * n_stn
     full = SPREAD * SPREAD * tiles
     strip = UV // n_grid
+    heights = [padded(stop - start) for _, start, stop in groups]
     summed = pl.pallas_call(
-        functools.partial(whole_kernel, dims),
+        functools.partial(whole_kernel, dims, groups),
         out_shape=jax.ShapeDtypeStruct((chans, strip, 2 * UV), f32),
-        in_specs=[anywhere, vmem, vmem, vmem, vmem, smem, smem],
+        in_specs=[anywhere, vmem, vmem, vmem, vmem, smem],
         out_specs=vmem,
         scratch_shapes=[
             pltpu.VMEM((LANES, taps * frame_len + samples), bf16),
             pltpu.VMEM((2 * n_stn * chans * STEP, reach), bf16),
-            pltpu.VMEM((chans, n_stn, 2, blocks, STEP, LANES), bf16),
-            pltpu.VMEM((chans, n_stn, ROWS, LANES), bf16),
+            pltpu.VMEM((2, n_stn, 2, 2, 2, STEP, chans * LANES), bf16),
             pltpu.VMEM((chans, n_stn, st, 2 * LANES), bf16),
             pltpu.VMEM((n_stn * 8, st, LANES), f32),
-            pltpu.VMEM((n_stn * 16, TILE * st), bf16),
+            pltpu.VMEM((n_stn * 8, TILE * st), bf16),
             pltpu.VMEM((TILE * st, 2 * LANES), bf16),
             pltpu.VMEM((n_stn, 16, LANES), bf16),
-            pltpu.VMEM((chans, n_stn, ROWS, LANES), bf16),
             pltpu.VMEM((n_stn, 16, LANES), bf16),
-            pltpu.VMEM((2, full + 48, n_stn * ROWS), bf16),
-            pltpu.VMEM((chans, SEPS, 2 * UV, PAIR_ROWS), bf16),
-            pltpu.VMEM((chans, 2, SPREAD, LANES, tiles * PATCH), bf16),
+            pltpu.VMEM((chans, 2 * UV, SEPS * PAIR_ROWS), bf16),
+            pltpu.VMEM((chans, 2, 2 * LANES, tiles * PATCH), bf16),
             pltpu.VMEM((chans, 2, LANES, tiles * PATCH), bf16),
             pltpu.VMEM((chans, PAIR_ROWS, LANES), f32),
             pltpu.VMEM((full + 48, 2 * LANES), bf16),
-            pltpu.VMEM((2, SPREAD, 2 * SEPS * tiles, LANES), bf16),
-            pltpu.VMEM((SEPS, PAIR_ROWS, 2 * UV), bf16),
+            pltpu.VMEM((4 * SEPS * tiles, 2 * LANES), bf16),
+            pltpu.VMEM((chans, SEPS * PAIR_ROWS, 2 * UV), bf16),
             pltpu.VMEM((chans, n_grid, strip, 2 * UV), bf16),
             pltpu.VMEM((chans, n_grid, strip, 2 * UV), bf16),
+            *[pltpu.VMEM((n_stn, h, LANES), bf16) for h in heights],
+            *[pltpu.VMEM((n_stn, h, LANES), bf16) for h in heights],
+            *[pltpu.VMEM((n_stn, h, LANES), f32) for h in heights],
             pltpu.SemaphoreType.DMA,
             pltpu.SemaphoreType.DMA,
             pltpu.SemaphoreType.DMA,
-            pltpu.SemaphoreType.DMA((chans, n_stn)),
-            pltpu.SemaphoreType.DMA((chans, n_stn)),
+            pltpu.SemaphoreType.DMA((len(groups), n_stn)),
+            pltpu.SemaphoreType.DMA((len(groups), n_stn)),
             pltpu.SemaphoreType.DMA((n_stn,)),
             pltpu.SemaphoreType.DMA((n_stn,)),
             pltpu.SemaphoreType.DMA((chans, n_grid)),
@@ -680,7 +758,7 @@
         compiler_params=pltpu.CompilerParams(
             collective_id=0, has_side_effects=True, vmem_limit_bytes=48 << 20
         ),
-    )(flat, pfb_coeffs, table, station_offsets, tile_cells, station_offsets, kernel_table)
+    )(flat, pfb_coeffs, table, station_offsets, tile_cells, kernel_table)
     return jnp.transpose(summed, (1, 0, 2))
 
 

time: 41.8 us -> 36.1 us (0.86)
  Pallas kernels: 38.9 us -> 33 us
  local copies, waits for them, and re-layouts: 2.51 us -> 2.98 us
    pallas_call x1, Pallas kernels: 38.9 us -> 33 us  [kernel_body(): pl.pallas_call(functools.partial(whole_kernel, dims, groups), out_shape=j...]
    reshape x1, local copies, waits for them, and re-layouts: 0.3 us -> 2.32 us  [kernel_body(): flat = voltages.reshape(st * pols, samples)]
    unnamed x11, local copies, waits for them, and re-layouts: 1.69 us -> 0.66 us
    another operation x4 -> x0, local copies, waits for them, and re-layouts: 0.53 us -> none  [kernel_body(): table = jnp.tile(table, (1, STEP + taps))]
where the time goes in v2:
time: 36.1 us; the launch traced here: 36 us
  Pallas kernels  33 us (91%)
  local copies, waits for them, and re-layouts  2.98 us (8%)
    pallas_call x1, Pallas kernels, kernel_body(): pl.pallas_call(functools.partial(whole_kernel, dims, groups), out_shape=j...  33 us
    reshape x1, local copies, waits for them, and re-layouts, kernel_body(): flat = voltages.reshape(st * pols, samples)  2.32 us

profile of v2, /device:TPU:0, one launch (start us, length us, event | category | flops | bytes accessed | tf_op | source)
XLA Modules:
  0.0 36.0 jit_solution(13838982109675157852)
XLA Ops:
  0.0 0.0 copy-start
  0.0 0.0 copy-start.4
  0.0 0.0 copy-start.2
  0.0 0.0 copy-start.3
  0.0 0.0 copy-start.1
  0.0 2.3 %reshape.3.v_ref = bf16[128,3072]{1,0:T(8,128)(2,1)S(1)} reshape(bf16[64,2,3072]{2,1,0:T(2,128)(2,1)} %param.6) | data formatting | bytes 1572864 | tf_op jit(solution)/shard_map/reshape | solution.py:716
  2.3 0.0 copy-done
  2.3 0.0 copy-done.4
  2.4 0.0 copy-done.2
  2.4 0.0 copy-done.3
  2.4 0.0 copy-done.1
  2.4 33.0 %shard_map.64 = f32[3,32,256]{2,1,0:T(8,128)S(1)} custom-call(bf16[128,3072]{1,0:T(8,128)(2,1)S(1)} %reshape.3.v_ref, f32[16,48]{1,0:T(8,128)S(1)} %copy-done.1, f32[48,1536]{1,0:T(8,128)S(1)} %copy-done, s32[2,512]{1,0:T(2,128)S(1)} %copy-done.3, s32[3,2,136]{2,1,0:T(2,128)S(1)} %copy-done.2, f32[8,7]{1,0:T(8,128)S(1)} %copy-done.4), custom_call_target="tpu_custom_call" | custom-call | tf_op jit(solution)/shard_map/pallas_call | solution.py:721
  35.4 0.6 %copy.8 = f32[32,3,256]{2,0,1:T(8,128)} copy(f32[32,3,256]{2,0,1:T(8,128)S(1)} %bitcast.1) | data formatting | bytes 196608
Async XLA Ops:
  0.0 2.3 %copy-start = (f32[48,1536]{1,0:T(8,128)S(1)}, f32[48,1536]{1,0:T(8,128)}, u32[]{:S(2)}) copy-start(f32[48,1536]{1,0:T(8,128)} %constant.2.clone.tw_ref) | copy-start | bytes 884740
  0.0 2.3 %copy-start.4 = (f32[8,7]{1,0:T(8,128)S(1)}, f32[8,7]{1,0:T(8,128)}, u32[]{:S(2)}) copy-start(f32[8,7]{1,0:T(8,128)} %table_ref.1) | copy-start | bytes 676
  0.0 2.4 %copy-start.2 = (s32[3,2,136]{2,1,0:T(2,128)S(1)}, s32[3,2,136]{2,1,0:T(2,128)}, u32[]{:S(2)}) copy-start(s32[3,2,136]{2,1,0:T(2,128)} %cells_ref.1) | copy-start | bytes 9796
  0.0 2.4 %copy-start.3 = (s32[2,512]{1,0:T(2,128)S(1)}, s32[2,512]{1,0:T(2,128)}, u32[]{:S(2)}) copy-start(s32[2,512]{1,0:T(2,128)} %off_ref.1) | copy-start | bytes 12292
  0.0 2.4 %copy-start.1 = (f32[16,48]{1,0:T(8,128)S(1)}, f32[16,48]{1,0:T(8,128)}, u32[]{:S(2)}) copy-start(f32[16,48]{1,0:T(8,128)} %coef_ref.1) | copy-start | bytes 9220

commit v3 on v2

--- a/solution.py
+++ b/solution.py
@@ -299,11 +299,11 @@
     cls = jnp.broadcast_to(SPREAD * offs[0:1] + offs[1:2], (16, stations)).astype(bf16)
     kap = jnp.broadcast_to(SEPS * offs[0:1] + offs[1:2], (LANES, stations)).astype(bf16)
     row_of = (stations, LANES)
-    mine = ones_where(iota(row_of, 0) == me * st + iota(row_of, 1) // 2)
+    mine = ones_where(iota(row_of, 0) == me * st + iota(row_of, 1) % st)
     cls_line = dot(cls, mine)[0:1]
     kap_line = dot(kap[:16], mine)[0:1]
     lane = iota((1, LANES), 1)
-    code = (lane // 2 // TILE).astype(f32) * CLASSES + cls_line
+    code = (lane % st // TILE).astype(f32) * CLASSES + cls_line
 
     def class_rows(start, stop):
         lines = iota((padded(stop - start), LANES), 0)
@@ -312,7 +312,7 @@
             [ones_where(lines == code + c * SUMS) for c in channels_of(start, stop)], axis=1
         )
 
-    own_rows = ones_where(iota((st, LANES), 0) == iota((st, LANES), 1) // 2)
+    own_rows = ones_where(iota((st, LANES), 0) == iota((st, LANES), 1) % st)
 
     pl.semaphore_wait(barrier, n_stn + n_grid - 2)
 
@@ -328,7 +328,7 @@
         ).start()
 
     load.wait()
-    even = iota((2 * n_stn * STEP, LANES), 1) % 2 == 0
+    even = iota((2 * n_stn * STEP, LANES), 1) < st
 
     def filtered(h, c):
         rows = wide[c * 2 * n_stn * STEP : (c + 1) * 2 * n_stn * STEP, :]
@@ -453,7 +453,7 @@
     row_t = iota((TILE, LANES), 0)
     for i in range(TILE):
         for a in range(2):
-            at = 2 * (a * TILE + i)
+            at = a * TILE + i
             value = kap_line[0:1, at : at + 1]
             hit = ones_where((base[a * TILE : (a + 1) * TILE] == value) & (row_t > i))
             first = i * st + a * TILE
@@ -484,6 +484,9 @@
     drecv_ref[me] = dsend[me]
     for k in order:
         sent(late[1], k)
+    for k in order:
+        sent(late[2], k)
+
 
     tiles = 2 * n_stn
     over, kern = table_ref.shape
@@ -550,9 +553,6 @@
             vweights[c, j, SEPS * tiles :, :] = jnp.zeros((depth - SEPS * tiles, across_w), bf16)
         for j, part in enumerate(split(across)):
             oweights[c, j] = jnp.where(own_block, dot(onto, part), 0.0).astype(bf16)
-
-    for k in order:
-        sent(late[2], k)
 
     ready = set()
     reduced = []
@@ -666,14 +666,12 @@
             copy.start()
             reduced.append(copy)
 
-    for c in range(chans - 1):
+    for c in range(chans):
         correlated(c)
-    for copy in own_arrivals:
-        copy.wait_recv()
-    for c in range(chans - 1):
+        if c == 0:
+            for copy in own_arrivals:
+                copy.wait_recv()
         gridded(c)
-    correlated(chans - 1)
-    gridded(chans - 1)
 
     for c in range(chans):
         total = rs_send[c, here].astype(f32)
@@ -713,7 +711,7 @@
     vmem = pl.BlockSpec(memory_space=pltpu.VMEM)
     smem = pl.BlockSpec(memory_space=pltpu.SMEM)
     anywhere = pl.BlockSpec(memory_space=pl.ANY)
-    flat = voltages.reshape(st * pols, samples)
+    flat = jnp.transpose(voltages, (1, 0, 2)).reshape(pols * st, samples)
     tiles = 2 * n_stn
     full = SPREAD * SPREAD * tiles
     strip = UV // n_grid

time: 36.1 us -> 34 us (0.942)
  Pallas kernels: 33 us -> 31.8 us
  local copies, waits for them, and re-layouts: 2.98 us -> 1.99 us
    reshape x1 -> x0, local copies, waits for them, and re-layouts: 2.32 us -> none  [kernel_body(): flat = voltages.reshape(st * pols, samples)]
    transpose x0 -> x1, local copies, waits for them, and re-layouts: none -> 1.32 us  [kernel_body(): flat = jnp.transpose(voltages, (1, 0, 2)).reshape(pols * st, samples)]
    pallas_call x1, Pallas kernels: 33 us -> 31.8 us  [kernel_body(): pl.pallas_call(functools.partial(whole_kernel, dims, groups), out_shape=j...]
where the time goes in v3:
time: 34 us; the launch traced here: 33.8 us
  Pallas kernels  31.8 us (94%)
  local copies, waits for them, and re-layouts  1.99 us (6%)
    pallas_call x1, Pallas kernels, kernel_body(): pl.pallas_call(functools.partial(whole_kernel, dims, groups), out_shape=j...  31.8 us
    transpose x1, local copies, waits for them, and re-layouts, kernel_body(): flat = jnp.transpose(voltages, (1, 0, 2)).reshape(pols * st, samples)  1.32 us

profile of v3, /device:TPU:0, one launch (start us, length us, event | category | flops | bytes accessed | tf_op | source)
XLA Modules:
  0.0 33.8 jit_solution(4576952948804929265)
XLA Ops:
  0.0 0.0 copy-start
  0.0 0.0 copy-start.1
  0.0 0.0 copy-start.2
  0.0 0.0 copy-start.3
  0.0 0.0 copy-start.4
  0.0 1.3 %copy.7 = bf16[2,64,3072]{2,1,0:T(8,128)(2,1)S(1)} copy(bf16[2,64,3072]{2,0,1:T(2,128)(2,1)} %bitcast.5) | data formatting | bytes 1572864 | tf_op jit(solution)/shard_map/transpose | solution.py:714
  1.3 0.0 copy-done
  1.4 0.0 copy-done.1
  1.4 0.0 copy-done.2
  1.4 0.0 copy-done.3
  1.4 0.0 copy-done.4
  1.4 31.8 %shard_map.64 = f32[3,32,256]{2,1,0:T(8,128)S(1)} custom-call(bf16[128,3072]{1,0:T(8,128)(2,1)S(1)} %bitcast.3, f32[16,48]{1,0:T(8,128)S(1)} %copy-done.1, f32[48,1536]{1,0:T(8,128)S(1)} %copy-done, s32[2,512]{1,0:T(2,128)S(1)} %copy-done.3, s32[3,2,136]{2,1,0:T(2,128)S(1)} %copy-done.2, f32[8,7]{1,0:T(8,128)S(1)} %copy-done.4), custom_call_target="tpu_custom_call" | custom-call | tf_op jit(solution)/shard_map/pallas_call | solution.py:719
  33.2 0.6 %copy.9 = f32[32,3,256]{2,0,1:T(8,128)} copy(f32[32,3,256]{2,0,1:T(8,128)S(1)} %bitcast.4) | data formatting | bytes 196608
Async XLA Ops:
  0.0 1.3 %copy-start = (f32[48,1536]{1,0:T(8,128)S(1)}, f32[48,1536]{1,0:T(8,128)}, u32[]{:S(2)}) copy-start(f32[48,1536]{1,0:T(8,128)} %constant.2.clone.tw_ref) | copy-start | bytes 884740
  0.0 1.4 %copy-start.1 = (f32[16,48]{1,0:T(8,128)S(1)}, f32[16,48]{1,0:T(8,128)}, u32[]{:S(2)}) copy-start(f32[16,48]{1,0:T(8,128)} %coef_ref.1) | copy-start | bytes 9220
  0.0 1.4 %copy-start.2 = (s32[3,2,136]{2,1,0:T(2,128)S(1)}, s32[3,2,136]{2,1,0:T(2,128)}, u32[]{:S(2)}) copy-start(s32[3,2,136]{2,1,0:T(2,128)} %cells_ref.1) | copy-start | bytes 9796
  0.0 1.4 %copy-start.3 = (s32[2,512]{1,0:T(2,128)S(1)}, s32[2,512]{1,0:T(2,128)}, u32[]{:S(2)}) copy-start(s32[2,512]{1,0:T(2,128)} %off_ref.1) | copy-start | bytes 12292
  0.0 1.4 %copy-start.4 = (f32[8,7]{1,0:T(8,128)S(1)}, f32[8,7]{1,0:T(8,128)}, u32[]{:S(2)}) copy-start(f32[8,7]{1,0:T(8,128)} %table_ref.1) | copy-start | bytes 676

commit v4 on v3

--- a/solution.py
+++ b/solution.py
@@ -254,13 +254,14 @@
     n_msg = len(groups)
     sends, recvs, flats = rest[:n_msg], rest[n_msg : 2 * n_msg], rest[2 * n_msg : 3 * n_msg]
     (
-        in_sem, halo_send, halo_recv, send_sem, recv_sem, dsend_sem, drecv_sem,
+        halo_send, halo_recv, send_sem, recv_sem, dsend_sem, drecv_sem,
         rs_send_sem, rs_recv_sem,
     ) = rest[3 * n_msg :]
     me, here = lax.axis_index("stn"), lax.axis_index("grid")
     reach = (STEP + taps) * frame_len
     halo = taps * frame_len
     samples = v_ref.shape[1]
+    stride = STEP * frame_len
     order = send_order(n_stn)
 
     barrier = pltpu.get_barrier_semaphore()
@@ -272,8 +273,6 @@
         pl.semaphore_signal(
             barrier, inc=1, device_id=(me, lax.rem(here + k, n_grid)), device_id_type=MESH
         )
-    load = pltpu.make_async_copy(v_ref, vext.at[:, pl.ds(halo, samples)], in_sem)
-    load.start()
 
     coef = coef_ref[...]
     line = jnp.concatenate(
@@ -327,16 +326,16 @@
             device_id_type=MESH,
         ).start()
 
-    load.wait()
+    vext[:, halo:] = v_ref[:, :stride]
     even = iota((2 * n_stn * STEP, LANES), 1) < st
 
     def filtered(h, c):
         rows = wide[c * 2 * n_stn * STEP : (c + 1) * 2 * n_stn * STEP, :]
-        first = 2 * h * STEP * frame_len
-        second = first + STEP * frame_len
-        window = jnp.concatenate(
-            [vext[:, first : first + reach], vext[:, second : second + reach]], axis=0
-        )
+        windows = [
+            v_ref[:, t * stride - halo : t * stride - halo + reach] if t else vext[...]
+            for t in (2 * h, 2 * h + 1)
+        ]
+        window = jnp.concatenate(windows, axis=0)
         got = dot_nt(rows, window)
         for t in range(2):
             part = got[:, t * LANES : (t + 1) * LANES]
@@ -398,6 +397,20 @@
     for m in early:
         made(m, True)
     kept(1)
+
+    which = (st, stations)
+    kap_col = dot_nt(ones_where(iota(which, 1) == me * st + iota(which, 0)), kap)
+    base = kap_col + iota((st, LANES), 1).astype(f32) - (SEPS * (SPREAD - 1) + SPREAD - 1)
+    blank = jnp.zeros((TILE, LANES), bf16)
+    row_t = iota((TILE, LANES), 0)
+    for i in range(TILE):
+        for a in range(2):
+            at = a * TILE + i
+            value = kap_line[0:1, at : at + 1]
+            hit = ones_where((base[a * TILE : (a + 1) * TILE] == value) & (row_t > i))
+            first = i * st + a * TILE
+            picks[first : first + TILE, a * LANES : (a + 1) * LANES] = hit
+            picks[first : first + TILE, (1 - a) * LANES : (2 - a) * LANES] = blank
 
     halo_copy = pltpu.make_async_remote_copy(
         src_ref=v_ref.at[:, pl.ds(samples - halo, halo)],
@@ -446,19 +459,6 @@
         first = jnp.where(lane3 % st < TILE, vis[:, 2 * k, :], vis[:, 2 * k + TILE, :])
         second = jnp.where(lane3 % st < TILE, vis[:, 2 * k + 1, :], vis[:, 2 * k + 1 + TILE, :])
         left[:, k * LANES : (k + 1) * LANES] = jnp.where(lane3 < st, first, second).astype(bf16)
-    which = (st, stations)
-    kap_col = dot_nt(ones_where(iota(which, 1) == me * st + iota(which, 0)), kap)
-    base = kap_col + iota((st, LANES), 1).astype(f32) - (SEPS * (SPREAD - 1) + SPREAD - 1)
-    blank = jnp.zeros((TILE, LANES), bf16)
-    row_t = iota((TILE, LANES), 0)
-    for i in range(TILE):
-        for a in range(2):
-            at = a * TILE + i
-            value = kap_line[0:1, at : at + 1]
-            hit = ones_where((base[a * TILE : (a + 1) * TILE] == value) & (row_t > i))
-            first = i * st + a * TILE
-            picks[first : first + TILE, a * LANES : (a + 1) * LANES] = hit
-            picks[first : first + TILE, (1 - a) * LANES : (2 - a) * LANES] = blank
     binned = dot(left[...], picks[...])
     dsend[...] = jnp.concatenate(
         [
@@ -635,7 +635,7 @@
                         bf16
                     )
 
-    def gridded(c):
+    def alone_placed(c):
         rr, cc = iota((32, n_stn * 16), 0), iota((32, n_stn * 16), 1)
         b = rr % tiles
         take = ones_where(cc == (b % n_stn) * 16 + (b // n_stn) * 8 + c * 2 + rr // tiles)
@@ -650,6 +650,8 @@
                 placed[c, first : first + tiles, e * LANES : (e + 1) * LANES] = jnp.where(
                     valid, moved, 0.0
                 ).astype(bf16)
+
+    def gridded(c):
         plane = dot(bands[c], placed[c])
         plane = (plane[:UV] + plane[UV:]) * norm
         rs_send[c] = plane.astype(bf16).reshape(n_grid, UV // n_grid, 2 * UV)
@@ -671,6 +673,8 @@
         if c == 0:
             for copy in own_arrivals:
                 copy.wait_recv()
+            for other in range(chans):
+                alone_placed(other)
         gridded(c)
 
     for c in range(chans):
@@ -710,7 +714,6 @@
     table = jnp.asarray(np.tile(table.reshape(-1, frame_len), (1, STEP + taps)))
     vmem = pl.BlockSpec(memory_space=pltpu.VMEM)
     smem = pl.BlockSpec(memory_space=pltpu.SMEM)
-    anywhere = pl.BlockSpec(memory_space=pl.ANY)
     flat = jnp.transpose(voltages, (1, 0, 2)).reshape(pols * st, samples)
     tiles = 2 * n_stn
     full = SPREAD * SPREAD * tiles
@@ -719,10 +722,10 @@
     summed = pl.pallas_call(
         functools.partial(whole_kernel, dims, groups),
         out_shape=jax.ShapeDtypeStruct((chans, strip, 2 * UV), f32),
-        in_specs=[anywhere, vmem, vmem, vmem, vmem, smem],
+        in_specs=[vmem, vmem, vmem, vmem, vmem, smem],
         out_specs=vmem,
         scratch_shapes=[
-            pltpu.VMEM((LANES, taps * frame_len + samples), bf16),
+            pltpu.VMEM((LANES, reach), bf16),
             pltpu.VMEM((2 * n_stn * chans * STEP, reach), bf16),
             pltpu.VMEM((2, n_stn, 2, 2, 2, STEP, chans * LANES), bf16),
             pltpu.VMEM((chans, n_stn, st, 2 * LANES), bf16),
@@ -745,7 +748,6 @@
             *[pltpu.VMEM((n_stn, h, LANES), f32) for h in heights],
             pltpu.SemaphoreType.DMA,
             pltpu.SemaphoreType.DMA,
-            pltpu.SemaphoreType.DMA,
             pltpu.SemaphoreType.DMA((len(groups), n_stn)),
             pltpu.SemaphoreType.DMA((len(groups), n_stn)),
             pltpu.SemaphoreType.DMA((n_stn,)),

time: 34 us -> 33.9 us (level)
  no operation moved by 1% of the time
where the time goes in v4:
time: 33.9 us; the launch traced here: 33.8 us
  Pallas kernels  31.7 us (94%)
  local copies, waits for them, and re-layouts  1.99 us (6%)
    pallas_call x1, Pallas kernels, kernel_body(): pl.pallas_call(functools.partial(whole_kernel, dims, groups), out_shape=j...  31.7 us
    transpose x1, local copies, waits for them, and re-layouts, kernel_body(): flat = jnp.transpose(voltages, (1, 0, 2)).reshape(pols * st, samples)  1.32 us

profile of v4, /device:TPU:0, one launch (start us, length us, event | category | flops | bytes accessed | tf_op | source)
XLA Modules:
  0.0 33.8 jit_solution(12256598786024823500)
XLA Ops:
  0.0 0.0 copy-start
  0.0 0.0 copy-start.1
  0.0 0.0 copy-start.2
  0.0 0.0 copy-start.3
  0.0 0.0 copy-start.4
  0.0 1.3 %copy.7 = bf16[2,64,3072]{2,1,0:T(8,128)(2,1)S(1)} copy(bf16[2,64,3072]{2,0,1:T(2,128)(2,1)} %bitcast.5) | data formatting | bytes 1572864 | tf_op jit(solution)/shard_map/transpose | solution.py:717
  1.3 0.0 copy-done
  1.4 0.0 copy-done.1
  1.4 0.0 copy-done.2
  1.4 0.0 copy-done.3
  1.4 0.0 copy-done.4
  1.4 31.7 %shard_map.64 = f32[3,32,256]{2,1,0:T(8,128)S(1)} custom-call(bf16[128,3072]{1,0:T(8,128)(2,1)S(1)} %bitcast.3, f32[16,48]{1,0:T(8,128)S(1)} %copy-done.1, f32[48,1536]{1,0:T(8,128)S(1)} %copy-done, s32[2,512]{1,0:T(2,128)S(1)} %copy-done.3, s32[3,2,136]{2,1,0:T(2,128)S(1)} %copy-done.2, f32[8,7]{1,0:T(8,128)S(1)} %copy-done.4), custom_call_target="tpu_custom_call" | custom-call | tf_op jit(solution)/shard_map/pallas_call | solution.py:722
  33.1 0.6 %copy.9 = f32[32,3,256]{2,0,1:T(8,128)} copy(f32[32,3,256]{2,0,1:T(8,128)S(1)} %bitcast.4) | data formatting | bytes 196608
Async XLA Ops:
  0.0 1.3 %copy-start = (f32[48,1536]{1,0:T(8,128)S(1)}, f32[48,1536]{1,0:T(8,128)}, u32[]{:S(2)}) copy-start(f32[48,1536]{1,0:T(8,128)} %constant.2.clone.tw_ref) | copy-start | bytes 884740
  0.0 1.4 %copy-start.1 = (f32[16,48]{1,0:T(8,128)S(1)}, f32[16,48]{1,0:T(8,128)}, u32[]{:S(2)}) copy-start(f32[16,48]{1,0:T(8,128)} %coef_ref.1) | copy-start | bytes 9220
  0.0 1.4 %copy-start.2 = (s32[3,2,136]{2,1,0:T(2,128)S(1)}, s32[3,2,136]{2,1,0:T(2,128)}, u32[]{:S(2)}) copy-start(s32[3,2,136]{2,1,0:T(2,128)} %cells_ref.1) | copy-start | bytes 9796
  0.0 1.4 %copy-start.3 = (s32[2,512]{1,0:T(2,128)S(1)}, s32[2,512]{1,0:T(2,128)}, u32[]{:S(2)}) copy-start(s32[2,512]{1,0:T(2,128)} %off_ref.1) | copy-start | bytes 12292
  0.0 1.4 %copy-start.4 = (f32[8,7]{1,0:T(8,128)S(1)}, f32[8,7]{1,0:T(8,128)}, u32[]{:S(2)}) copy-start(f32[8,7]{1,0:T(8,128)} %table_ref.1) | copy-start | bytes 676

commit v5 on v4

--- a/solution.py
+++ b/solution.py
@@ -682,7 +682,7 @@
         for k in range(1, n_grid):
             reduced[c * (n_grid - 1) + k - 1].wait_recv()
             total = total + rs_recv[c, k].astype(f32)
-        out_ref[c] = total
+        out_ref[:, c, :] = total
     for copy in copies + reduced:
         copy.wait_send()
 
@@ -721,7 +721,7 @@
     heights = [padded(stop - start) for _, start, stop in groups]
     summed = pl.pallas_call(
         functools.partial(whole_kernel, dims, groups),
-        out_shape=jax.ShapeDtypeStruct((chans, strip, 2 * UV), f32),
+        out_shape=jax.ShapeDtypeStruct((strip, chans, 2 * UV), f32),
         in_specs=[vmem, vmem, vmem, vmem, vmem, smem],
         out_specs=vmem,
         scratch_shapes=[
@@ -759,7 +759,7 @@
             collective_id=0, has_side_effects=True, vmem_limit_bytes=48 << 20
         ),
     )(flat, pfb_coeffs, table, station_offsets, tile_cells, kernel_table)
-    return jnp.transpose(summed, (1, 0, 2))
+    return summed
 
 
 def kernels_fit(mesh, args):

time: 33.9 us -> 33.9 us (level)
    pallas_call x0 -> x1, local copies, waits for them, and re-layouts: none -> 0.66 us  [kernel_body(): pl.pallas_call(functools.partial(whole_kernel, dims, groups), out_shape=j...]
    unnamed x11 -> x10, local copies, waits for them, and re-layouts: 0.66 us -> 0.02 us
where the time goes in v5:
time: 33.9 us; the launch traced here: 33.8 us
  Pallas kernels  31.7 us (94%)
  local copies, waits for them, and re-layouts  2 us (6%)
    pallas_call x1, Pallas kernels, kernel_body(): pl.pallas_call(functools.partial(whole_kernel, dims, groups), out_shape=j...  31.7 us
    transpose x1, local copies, waits for them, and re-layouts, kernel_body(): flat = jnp.transpose(voltages, (1, 0, 2)).reshape(pols * st, samples)  1.32 us

profile of v5, /device:TPU:0, one launch (start us, length us, event | category | flops | bytes accessed | tf_op | source)
XLA Modules:
  0.0 33.8 jit_solution(10339772159590358720)
XLA Ops:
  0.0 0.0 copy-start
  0.0 0.0 copy-start.1
  0.0 0.0 copy-start.2
  0.0 0.0 copy-start.3
  0.0 0.0 copy-start.4
  0.0 1.3 %copy.7 = bf16[2,64,3072]{2,1,0:T(8,128)(2,1)S(1)} copy(bf16[2,64,3072]{2,0,1:T(2,128)(2,1)} %bitcast.3) | data formatting | bytes 1572864 | tf_op jit(solution)/shard_map/transpose | solution.py:717
  1.3 0.0 copy-done
  1.4 0.0 copy-done.1
  1.4 0.0 copy-done.2
  1.4 0.0 copy-done.3
  1.4 0.0 copy-done.4
  1.4 31.7 %shard_map.64 = f32[32,3,256]{2,1,0:T(4,128)S(1)} custom-call(bf16[128,3072]{1,0:T(8,128)(2,1)S(1)} %bitcast.2, f32[16,48]{1,0:T(8,128)S(1)} %copy-done.1, f32[48,1536]{1,0:T(8,128)S(1)} %copy-done, s32[2,512]{1,0:T(2,128)S(1)} %copy-done.3, s32[3,2,136]{2,1,0:T(2,128)S(1)} %copy-done.2, f32[8,7]{1,0:T(8,128)S(1)} %copy-done.4), custom_call_target="tpu_custom_call" | custom-call | tf_op jit(solution)/shard_map/pallas_call | solution.py:722
  33.1 0.7 %copy.8 = f32[32,3,256]{2,0,1:T(8,128)} copy(f32[32,3,256]{2,1,0:T(4,128)S(1)} %shard_map.64) | data formatting | bytes 196608 | tf_op jit(solution)/shard_map/pallas_call | solution.py:722
Async XLA Ops:
  0.0 1.3 %copy-start = (f32[48,1536]{1,0:T(8,128)S(1)}, f32[48,1536]{1,0:T(8,128)}, u32[]{:S(2)}) copy-start(f32[48,1536]{1,0:T(8,128)} %constant.2.clone.tw_ref) | copy-start | bytes 884740
  0.0 1.4 %copy-start.1 = (f32[16,48]{1,0:T(8,128)S(1)}, f32[16,48]{1,0:T(8,128)}, u32[]{:S(2)}) copy-start(f32[16,48]{1,0:T(8,128)} %coef_ref.1) | copy-start | bytes 9220
  0.0 1.4 %copy-start.2 = (s32[3,2,136]{2,1,0:T(2,128)S(1)}, s32[3,2,136]{2,1,0:T(2,128)}, u32[]{:S(2)}) copy-start(s32[3,2,136]{2,1,0:T(2,128)} %cells_ref.1) | copy-start | bytes 9796
  0.0 1.4 %copy-start.3 = (s32[2,512]{1,0:T(2,128)S(1)}, s32[2,512]{1,0:T(2,128)}, u32[]{:S(2)}) copy-start(s32[2,512]{1,0:T(2,128)} %off_ref.1) | copy-start | bytes 12292
  0.0 1.4 %copy-start.4 = (f32[8,7]{1,0:T(8,128)S(1)}, f32[8,7]{1,0:T(8,128)}, u32[]{:S(2)}) copy-start(f32[8,7]{1,0:T(8,128)} %table_ref.1) | copy-start | bytes 676
